TPU v7x, 128 devices: a whole 4x4x4 slice. The times are simulated.
128 devices in a mesh: batch: 32 (over y, x, core), seq: 4 (over z).
Axes of the slice: x: 4, y: 4, z: 4, core: 2. Of those that a mesh axis runs over, the one named last changes fastest.
Arguments:
- token_ids: int32 [96, 512], P('batch', 'seq'), may hold values from 0 to 500735, as said below
- lengths: int32 [96], P('batch'), may hold values from 128 to 512, as said below
- word_table: bfloat16 [500736, 768], P(('batch', 'seq')), may hold values from -6 to 6
- positions: bfloat16 [512, 768], P('seq'), may hold values from -3 to 3
- query_weight: bfloat16 [768, 768], replicated, may hold values from -0.21875 to 0.21875
- key_weight: bfloat16 [768, 768], replicated, may hold values from -0.21875 to 0.21875
- value_weight: bfloat16 [768, 768], replicated, may hold values from -0.21875 to 0.21875
- query_bias: bfloat16 [768], replicated, may hold values from -1.75 to 1.75
- value_bias: bfloat16 [768], replicated, may hold values from -1.75 to 1.75
- output_weight: bfloat16 [768, 768], replicated, may hold values from -1.25 to 1.25
- output_bias: bfloat16 [768], replicated, may hold values from -1.75 to 1.75
- first_gain: bfloat16 [768], replicated, may hold values from 0.5 to 1.5
- first_shift: bfloat16 [768], replicated, may hold values from -1.75 to 1.75
- inner_weight: bfloat16 [768, 3072], replicated, may hold values from -0.21875 to 0.21875
- inner_bias: bfloat16 [3072], replicated, may hold values from -1.75 to 1.75
- outer_weight: bfloat16 [3072, 768], replicated, may hold values from -0.109375 to 0.109375
- outer_bias: bfloat16 [768], replicated, may hold values from -1.75 to 1.75
- second_gain: bfloat16 [768], replicated, may hold values from 0.5 to 1.5
- second_shift: bfloat16 [768], replicated, may hold values from -1.75 to 1.75
- pooler_weight: bfloat16 [768, 768], replicated, may hold values from -0.21875 to 0.21875
- pooler_bias: bfloat16 [768], replicated, may hold values from -1.75 to 1.75
- out_grad: bfloat16 [96, 512, 768], P('batch', 'seq'), may hold values from -6 to 6
- pooled_grad: float32 [96, 768], P('batch', 'seq'), may hold values from -6 to 6
Outputs:
- hidden_out: bfloat16 [96, 512, 768], P('batch', 'seq')
- pooled: float32 [96, 768], P('batch', 'seq')
- grad_table: float32 [500736, 768], P(('batch', 'seq'))
- grad_positions: float32 [512, 768], P('seq')
- grad_query_weight: float32 [768, 768], P('seq')
- grad_key_weight: float32 [768, 768], P('seq')
- grad_value_weight: float32 [768, 768], P('seq')
- grad_query_bias: float32 [768], P('seq')
- grad_value_bias: float32 [768], P('seq')
- grad_output_weight: float32 [768, 768], P('seq')
- grad_output_bias: float32 [768], P('seq')
- grad_first_gain: float32 [768], P('seq')
- grad_first_shift: float32 [768], P('seq')
- grad_inner_weight: float32 [768, 3072], P('seq')
- grad_inner_bias: float32 [3072], P('seq')
- grad_outer_weight: float32 [3072, 768], P('seq')
- grad_outer_bias: float32 [768], P('seq')
- grad_second_gain: float32 [768], P('seq')
- grad_second_shift: float32 [768], P('seq')
- grad_pooler_weight: float32 [768, 768], P('seq')
- grad_pooler_bias: float32 [768], P('seq')
Inputs may be any that keep to these rules, and one draw needn't show every extreme that they name: `token_ids`: on the tokens of one device (one index of batch and of seq), no range of 3912 consecutive table rows that one device holds is named by more than 6 tokens, and some ranges are named by exactly 6 tokens of every device. `lengths`: among the 3 sentences of each index of batch, at least one has length 512.
All inputs are finite; a program needn't handle non-finite values.
Results may differ from a plain program's by a relative error of at most 0.02.
Values may be sent and summed in bfloat16 or wider, within the bound.
No kernel may reach another device: no remote copies, remote signals or barrier semaphores. Data moves between devices by JAX's collectives and lax.ppermute only.
A program may use at most 256 MiB of HBM per device.

v0:
```python
import functools
import jax
import jax.numpy as jnp
from jax import lax
from jax.experimental import pallas as pl
from jax.experimental.pallas import tpu as pltpu
from jax.sharding import PartitionSpec as P

F32 = jnp.float32
LOW = jnp.bfloat16
EPSILON = 1e-12
MASKED = -1000000000.0
HEAD_DIM = 64
VMEM = 56 * 1024 * 1024
HALF = 384
SHARE = 0.02


def nn(a, b):
    return lax.dot_general(a, b, (((1,), (0,)), ((), ())), preferred_element_type=F32)


def nt(a, b):
    return lax.dot_general(a, b, (((1,), (1,)), ((), ())), preferred_element_type=F32)


def struct(shape, dtype):
    return jax.ShapeDtypeStruct(shape, dtype)


def whole(shape):
    zeros = (0,) * len(shape)
    return pl.BlockSpec(shape, lambda *_: zeros, pipeline_mode=pl.Buffered(1))


def cost(flops, size):
    return pl.CostEstimate(
        flops=int(flops * SHARE), bytes_accessed=int(size * SHARE), transcendentals=0
    )


def params(**kw):
    return pltpu.CompilerParams(vmem_limit_bytes=VMEM, **kw)


def attn_fwd_kernel(
    x0, x1, x2, x3, wq, wk, wv, bq, bv, live, x_o, q_o, k_o, v_o, e_o, inv_o, mt_o, mixed_o, x
):
    scale = HEAD_DIM ** (-0.5)
    n = x0.shape[0]

    @pl.when(pl.program_id(0) == 0)
    def _():
        for m, part in enumerate((x0, x1, x2, x3)):
            x[m * n : m * n + n, :] = part[...]
            x_o[m * n : m * n + n, :] = part[...]

    q = ((nn(x[...], wq[...]) + bq[...].astype(F32)) * scale).astype(LOW)
    q_o[...] = q
    k = nn(x[...], wk[...]).astype(LOW)
    k_o[...] = k
    v = nn(x[...], wv[...]) + bv[...].astype(F32)
    v_o[...] = v.astype(LOW)
    keep = live[...] > 0.0
    lane = lax.broadcasted_iota(jnp.int32, (1, 128), 1)
    for pair in range(q.shape[1] // 128):
        cols = slice(128 * pair, 128 * pair + 128)
        q2, k2 = q[:, cols], k[:, cols]
        vt = v[:, cols].T.astype(LOW)
        parts = []
        for h in range(2):
            kz = jnp.where((lane // 64) == h, k2, jnp.zeros((), LOW))
            s = nt(kz, q2)
            s = jnp.where(keep, s, MASKED)
            e = jnp.exp(s - jnp.max(s, axis=0, keepdims=True))
            inv = 1.0 / jnp.sum(e, axis=0, keepdims=True)
            eb = e.astype(LOW)
            e_o[2 * pair + h] = eb
            inv_o[2 * pair + h] = inv
            parts.append(nn(vt[64 * h : 64 * h + 64], eb) * inv)
        mt = jnp.concatenate(parts, axis=0)
        mt_o[cols, :] = mt.astype(LOW)
        mixed_o[:, cols] = mt.T.astype(LOW)


def attn_fwd(parts, wq, wk, wv, bq, bv, live, group=256):
    n, d = parts[0].shape
    s = 4 * n
    hg = group // HEAD_DIM
    col = pl.BlockSpec((s, group), lambda h: (0, h))
    wcol = pl.BlockSpec((d, group), lambda h: (0, h))
    brow = pl.BlockSpec((1, group), lambda h: (0, h))
    heads = d // HEAD_DIM
    return pl.pallas_call(
        attn_fwd_kernel,
        grid=(d // group,),
        in_specs=[whole((n, d))] * 4 + [wcol, wcol, wcol, brow, brow, whole((s, 1))],
        out_specs=[
            whole((s, d)),
            col,
            col,
            col,
            pl.BlockSpec((hg, s, s), lambda h: (h, 0, 0)),
            pl.BlockSpec((hg, 1, s), lambda h: (h, 0, 0)),
            pl.BlockSpec((group, s), lambda h: (h, 0)),
            col,
        ],
        out_shape=[
            struct((s, d), LOW),
            struct((s, d), LOW),
            struct((s, d), LOW),
            struct((s, d), LOW),
            struct((heads, s, s), LOW),
            struct((heads, 1, s), F32),
            struct((d, s), LOW),
            struct((s, d), LOW),
        ],
        scratch_shapes=[pltpu.VMEM((s, d), LOW)],
        compiler_params=params(),
        cost_estimate=cost(6 * s * d * d + 4 * s * s * 256 * heads, 16e6),
        name="attention_forward",
    )(*parts, wq, wk, wv, bq, bv, live)


def attn_bwd_heads(al, wo, q, k, v, e_i, inv_i, mt_i, dm, dq, dk, dv):
    step = pl.program_id(0)

    @pl.when(step == 0)
    def _():
        dm[...] = nt(al[...], wo[...]).astype(LOW)

    lane = lax.broadcasted_iota(jnp.int32, (1, 128), 1)
    cols = pl.ds(pl.multiple_of(step * 128, 128), 128)
    q2, k2, v2 = q[...], k[...], v[...]
    dmt = dm[:, cols].astype(F32).T
    kt = k2.astype(F32).T.astype(LOW)
    prod = dmt * mt_i[...].astype(F32)
    inv2 = [inv_i[h] for h in range(2)]
    dots = jnp.concatenate([dmt[64 * h : 64 * h + 64] * inv2[h] for h in range(2)], axis=0)
    dot_low = dots.astype(LOW)
    dout = dots.T.astype(LOW)
    dqt, dk2, dv2 = [], [], []
    for h in range(2):
        mine = (lane // 64) == h
        e = e_i[h]
        delta = jnp.sum(prod[64 * h : 64 * h + 64], axis=0, keepdims=True) * inv2[h]
        vz = jnp.where(mine, v2, jnp.zeros((), LOW))
        dp = nn(vz, dot_low)
        ds = (e.astype(F32) * (dp - delta)).astype(LOW)
        dv2.append(nn(e, dout))
        dk2.append(nn(ds, q2))
        dqt.append(nn(kt[64 * h : 64 * h + 64], ds))
    first = lane < 64
    dv[:, cols] = jnp.where(first, dv2[0], dv2[1]).astype(LOW)
    dk[:, cols] = jnp.where(first, dk2[0], dk2[1]).astype(LOW)
    dq[:, cols] = jnp.concatenate(dqt, axis=0).T.astype(LOW)


def embed_part(dq, dk, dv, wq, wk, wv, rows):
    return (
        nt(dq[rows, :], wq[...]) * HEAD_DIM ** (-0.5) + nt(dk[rows, :], wk[...]) + nt(dv[rows, :], wv[...])
    )


def attn_bwd_kernel(
    place, al, wo, q, k, v, e_i, inv_i, mt_i, wq_a, wk_a, wv_a, x_a, base_a, mixed_a,
    pool, vec1, vec2, ib, p0, p1, p2, p3, send, keep,
    dm, dq, dk, dv, wq, wk, wv, x, base, mixed, eg, sems
):
    pairs = ((wq_a, wq), (wk_a, wk), (wv_a, wv), (x_a, x), (base_a, base), (mixed_a, mixed))
    loads = [pltpu.make_async_copy(a, b, sems.at[i]) for i, (a, b) in enumerate(pairs)]

    @pl.when(pl.program_id(0) == 0)
    def _():
        for load in loads:
            load.start()

    attn_bwd_heads(al, wo, q, k, v, e_i, inv_i, mt_i, dm, dq, dk, dv)

    @pl.when(pl.program_id(0) == pl.num_programs(0) - 1)
    def _():
        for load in loads:
            load.wait()
        scale = HEAD_DIM ** (-0.5)
        s, d = base.shape
        n, share = s // 4, d // 4
        core = place[1]

        def put(owner, at, values):
            for c in range(2):

                @pl.when(core == c)
                def _():
                    out = keep if owner == c else send
                    for z in range(4):
                        out[z, at, :] = values(z)

        pieces = ((x, dq, scale), (x, dk, 1.0), (x, dv, 1.0), (mixed, al, 1.0))
        for i, (left, right, factor) in enumerate(pieces):
            weight = (tn(left[...], right[...]) * factor).astype(LOW)
            start = share * (i % 2)
            put(i // 2, slice(start, start + share), lambda z: weight[share * z : share * z + share])
        for m, part in enumerate((p0, p1, p2, p3)):
            at = slice(m * n, m * n + n)
            value = (base[at, :] + embed_part(dq, dk, dv, wq, wk, wv, at)).astype(LOW)
            eg[m] = value
            part[n : n + 16, :] = pool[...]
            part[0:n, :] = value
        put(0, slice(2 * share, 2 * share + n), lambda z: eg[(place[0] + 4 - z) % 4])
        vectors = [
            jnp.sum(dq[...].astype(F32), axis=0, keepdims=True) * scale,
            jnp.sum(dv[...].astype(F32), axis=0, keepdims=True),
            vec1[2:3, :],
            vec1[0:1, :],
            vec1[1:2, :],
            vec2[2:3, :],
            vec2[0:1, :],
            vec2[1:2, :],
        ]
        vectors += [ib[f] for f in range(4)] + [jnp.zeros((n - 12, d), F32)]
        vectors = jnp.concatenate(vectors, axis=0).astype(LOW)
        put(1, slice(2 * share, 2 * share + n), lambda z: vectors)


def attn_bwd(place, al, wo, q, k, v, e, inv, mt, wq, wk, wv, x, base, mixed, pool, vec1, vec2, ib):
    s, d = q.shape
    steps = d // 128
    heads = d // HEAD_DIM
    col = pl.BlockSpec((s, 128), lambda h, p: (0, h))
    small = [whole(pool.shape), whole(vec1.shape), whole(vec2.shape), whole(ib.shape)]
    ins = [
        whole((s, d)),
        whole((d, d)),
        col,
        col,
        col,
        pl.BlockSpec((2, s, s), lambda h, p: (h, 0, 0)),
        pl.BlockSpec((2, 1, s), lambda h, p: (h, 0, 0)),
        pl.BlockSpec((128, s), lambda h, p: (h, 0)),
    ]
    shapes = [((s // 4 + 16, d), LOW)] * 4 + [((4, d // 2 + s // 4, d), LOW)] * 2
    return pl.pallas_call(
        attn_bwd_kernel,
        grid_spec=prefetch(
            1,
            (steps,),
            ins + [pl.BlockSpec(memory_space=pl.ANY)] * 6 + small,
            [whole(shape) for shape, _ in shapes],
            [pltpu.VMEM((s, d), LOW)] * 4
            + [pltpu.VMEM((d, d), LOW)] * 3
            + [pltpu.VMEM((s, d), LOW), pltpu.VMEM((s, d), F32), pltpu.VMEM((s, d), LOW)]
            + [pltpu.VMEM((4, s // 4, d), LOW), pltpu.SemaphoreType.DMA((6,))],
        ),
        out_shape=[struct(*one) for one in shapes],
        compiler_params=params(),
        cost_estimate=cost(14 * s * d * d + 8 * s * s * 256 * heads, 28e6),
        name="attention_backward",
    )(place, al, wo, q, k, v, e, inv, mt, wq, wk, wv, x, base, mixed, pool, vec1, vec2, ib)


def normalize(values):
    center = values - jnp.mean(values, axis=-1, keepdims=True)
    root = lax.rsqrt(jnp.mean(center * center, axis=-1, keepdims=True) + EPSILON)
    return center * root, root


def normalize_back(upstream, normed, root, gain):
    scaled = upstream * gain
    plain = jnp.mean(scaled, axis=-1, keepdims=True)
    crossed = jnp.mean(scaled * normed, axis=-1, keepdims=True)
    return root * (scaled - plain - normed * crossed)


def gelu_pair(v):
    cdf = lax.erf(v * 0.7071067811865476) * 0.5 + 0.5
    bell = jnp.exp(v * v * -0.5)
    return v * cdf, cdf + v * (bell * 0.3989422804014327)


def ff_kernel(
    row0, mixed, wo, bo, x, g1, s1, w1, b1, w2, b2, g2, s2, wp, bp, u0, u1, u2, u3,
    lhs_o, rhs_o, t0, t1, t2, t3, pool_o, al_o, fb_o, vec1_o, vec2_o, ib_o,
    w1s, w2s, wps, ups, gp, normed1, acc, sb, sems, *, chunk
):
    s, d = x.shape
    blocks = w1s.shape[0]
    ol_o, hid_o = lhs_o.at[0], lhs_o.at[1]
    act_o, il_o = rhs_o.at[0], rhs_o.at[1]
    n = s // 4
    per = chunk // n
    outs = (t0, t1, t2, t3)
    chunks = [slice(r, r + chunk) for r in range(0, s, chunk)]

    def load1(f):
        return pltpu.make_async_copy(w1.at[:, pl.ds(f * d, d)], w1s.at[f], sems.at[f])

    def load2(f):
        return pltpu.make_async_copy(w2.at[pl.ds(f * d, d), :], w2s.at[f], sems.at[blocks + f])

    loads = [pltpu.make_async_copy(wp, wps, sems.at[2 * blocks])]
    for m, part in enumerate((u0, u1, u2, u3)):
        loads.append(pltpu.make_async_copy(part, ups.at[m], sems.at[2 * blocks + 1 + m]))
    for f in range(blocks):
        load1(f).start()
        load2(f).start()
    for load in loads:
        load.start()

    roots1 = []
    for rows in chunks:
        val = nn(mixed[rows, :], wo[...]) + bo[...].astype(F32) + x[rows, :].astype(F32)
        normed, root = normalize(val)
        roots1.append(root)
        normed1[rows, :] = normed
        h = (normed * g1[...].astype(F32) + s1[...].astype(F32)).astype(LOW)
        hid_o[rows, :] = h
        acc[rows, :] = h.astype(F32) + b2[...].astype(F32)

    def forward(f, carry):
        load1(f).wait()
        load2(f).wait()
        for rows in chunks:
            pre = nn(hid_o[rows, :], w1s[f]) + b1[f].astype(F32)
            act, slope = gelu_pair(pre)
            act = act.astype(LOW)
            act_o[f, rows, :] = act
            gp[f, rows, :] = slope.astype(LOW)
            acc[rows, :] += nn(act, w2s[f])
        return carry

    lax.fori_loop(0, blocks, forward, 0)
    for load in loads:
        load.wait()

    gain = g2[...].astype(F32)
    roots2 = []
    for k, rows in enumerate(chunks):
        normed, root = normalize(acc[rows, :])
        roots2.append(root)
        res = (normed * gain + s2[...].astype(F32)).astype(LOW)
        al_o[rows, :] = res
        for j in range(per):
            outs[k * per + j][...] = res[j * n : j * n + n, :]
        acc[rows, :] = normed
    cls = al_o[pl.ds(pl.multiple_of(row0[0], 128), 16), :]
    pooled = jnp.tanh(nn(cls, wps[...]) + bp[...].astype(F32))
    pull = 0.0
    for m in range(4):
        terms = ups[m, n : n + 16, :].astype(F32)
        terms = jnp.broadcast_to(terms[0:1] + terms[1:2], (8, d))
        pull = pull + pltpu.roll(terms, ((row0[2] + 4 - m) % 4) * (d // 4), 1)
    pre = pull[:1] * (1.0 - pooled * pooled)
    cls_grad = nt(pre.astype(LOW), wps[...])[:1]
    high = pooled[:1].astype(LOW).astype(F32)
    pool = [cls[:1].astype(F32), pre[:1], high, pooled[:1] - high, jnp.zeros((12, d), F32)]
    pool_o[...] = jnp.concatenate(pool, axis=0).astype(LOW)
    gs, ss, bs = 0.0, 0.0, 0.0
    for k, rows in enumerate(chunks):
        ids = lax.broadcasted_iota(jnp.int32, (chunk, 1), 0) + rows.start
        up = jnp.concatenate([ups[k * per + j, 0:n, :] for j in range(per)], axis=0).astype(F32)
        upstream = up + jnp.where(ids == row0[0], cls_grad, 0.0)
        normed = acc[rows, :]
        back = normalize_back(upstream, normed, roots2[k], gain)
        sb[rows, :] = back
        low = back.astype(LOW)
        ol_o[rows, :] = low
        gs = gs + jnp.sum(upstream * normed, axis=0, keepdims=True)
        ss = ss + jnp.sum(upstream, axis=0, keepdims=True)
        bs = bs + jnp.sum(low.astype(F32), axis=0, keepdims=True)
    live = row0[1].astype(F32)
    vec2_o[0:1, :] = gs * live
    vec2_o[1:2, :] = ss * live
    vec2_o[2:3, :] = bs * live

    def backward(f, carry):
        bias = 0.0
        for rows in chunks:
            low = (nt(ol_o[rows, :], w2s[f]) * gp[f, rows, :].astype(F32)).astype(LOW)
            il_o[f, rows, :] = low
            bias = bias + jnp.sum(low.astype(F32), axis=0, keepdims=True)
            sb[rows, :] += nt(low, w1s[f])
        ib_o[f] = bias
        return carry

    lax.fori_loop(0, blocks, backward, 0)
    gain = g1[...].astype(F32)
    gs, ss, bs = 0.0, 0.0, 0.0
    for k, rows in enumerate(chunks):
        upstream = sb[rows, :]
        normed = normed1[rows, :]
        back = normalize_back(upstream, normed, roots1[k], gain)
        fb_o[rows, :] = back
        low = back.astype(LOW)
        al_o[rows, :] = low
        gs = gs + jnp.sum(upstream * normed, axis=0, keepdims=True)
        ss = ss + jnp.sum(upstream, axis=0, keepdims=True)
        bs = bs + jnp.sum(low.astype(F32), axis=0, keepdims=True)
    vec1_o[0:1, :] = gs
    vec1_o[1:2, :] = ss
    vec1_o[2:3, :] = bs


def feed_forward(row0, mixed, wo, bo, x, g1, s1, w1, b1, w2, b2, g2, s2, wp, bp, ups, chunk=256):
    s, d = x.shape
    ff = w1.shape[1]
    blocks = ff // d
    full, row = whole((s, d)), whole((1, d))
    away = pl.BlockSpec(memory_space=pl.ANY)
    part = (s // 4 + 16, d)
    return pl.pallas_call(
        functools.partial(ff_kernel, chunk=chunk),
        grid_spec=prefetch(
            1,
            (1,),
            [full, whole((d, d)), row, full, row, row, away, whole((blocks, 1, d)), away, row, row, row]
            + [away, row]
            + [away] * 4,
            [whole((2, s, d)), whole((2, blocks, s, d))]
            + [whole((s // 4, d))] * 4
            + [whole((16, d)), full, full, whole((8, d)), whole((8, d)), whole((blocks, 1, d))],
            [
                pltpu.VMEM((blocks, d, d), LOW),
                pltpu.VMEM((blocks, d, d), LOW),
                pltpu.VMEM((d, d), LOW),
                pltpu.VMEM((4,) + part, LOW),
                pltpu.VMEM((blocks, s, d), LOW),
                pltpu.VMEM((s, d), F32),
                pltpu.VMEM((s, d), F32),
                pltpu.VMEM((s, d), F32),
                pltpu.SemaphoreType.DMA((2 * blocks + 5,)),
            ],
        ),
        out_shape=[struct((2, s, d), LOW), struct((2, blocks, s, d), LOW)]
        + [struct((s // 4, d), LOW)] * 4
        + [
            struct((16, d), LOW),
            struct((s, d), LOW),
            struct((s, d), F32),
            struct((8, d), F32),
            struct((8, d), F32),
            struct((blocks, 1, d), F32),
        ],
        compiler_params=params(),
        cost_estimate=cost(2 * s * d * d + 8 * s * d * ff, 30e6),
        name="feed_forward",
    )(row0, mixed, wo, bo, x, g1, s1, w1, b1.reshape(blocks, 1, d), w2, b2, g2, s2, wp, bp, *ups)


def tn(a, b):
    return lax.dot_general(a, b, (((0,), (0,)), ((), ())), preferred_element_type=F32)


def prefetch(count, grid, in_specs, out_specs, scratch=()):
    return pltpu.PrefetchScalarGridSpec(
        num_scalar_prefetch=count,
        grid=grid,
        in_specs=in_specs,
        out_specs=out_specs,
        scratch_shapes=list(scratch),
    )


def index_kernel(ids, req_o, col_o, row_o, *, rows, slots):
    count, n = ids.shape
    owners = req_o.shape[0]
    owner = ((ids[...].astype(F32) + 0.5) * (1.0 / rows)).astype(jnp.int32)
    local = ids[...] - owner * rows + 1
    flat = [owner.astype(F32), (local // 64).astype(F32), (local % 64).astype(F32)]
    flat = jnp.concatenate(flat + [jnp.zeros((16 - 3 * count, n), F32)], axis=0)
    cols = flat.T
    lane = lax.broadcasted_iota(jnp.int32, (n, owners), 1).astype(F32)
    before = lax.broadcasted_iota(jnp.int32, (n, n), 1) < lax.broadcasted_iota(jnp.int32, (n, n), 0)
    before = jnp.where(before, 1.0, 0.0).astype(LOW)
    seen = jnp.zeros((1, owners), F32)
    high, low, places = 0.0, 0.0, []
    slot_lane = lax.broadcasted_iota(jnp.int32, (n, 128), 1).astype(F32)
    for s in range(count):
        hot = jnp.where(lane == cols[:, s : s + 1], 1.0, 0.0)
        hot_low = hot.astype(LOW)
        within = jnp.sum((nn(before, hot_low) + seen) * hot, axis=1, keepdims=True)
        seen = seen + jnp.sum(hot, axis=0, keepdims=True)
        place = cols[:, s : s + 1] * slots + within
        places.append(place)
        here = slot_lane == within
        put_high = jnp.where(here, cols[:, count + s : count + s + 1], 0.0).astype(LOW)
        put_low = jnp.where(here, cols[:, 2 * count + s : 2 * count + s + 1], 0.0).astype(LOW)
        high = high + tn(hot_low, put_high)
        low = low + tn(hot_low, put_low)
    req_o[...] = (high * 64.0 + low).astype(jnp.int32)[:, :slots] - 1
    places.append(jnp.full((n, 1), -1.0, F32))
    table = jnp.concatenate([jnp.broadcast_to(p, (n, 8)) for p in places], axis=1)
    table = jnp.concatenate([table, jnp.zeros((n, 128 - table.shape[1]), F32)], axis=1)
    turned = table.T.astype(jnp.int32)
    for s in range(count + 1):
        col_o[s] = places[s].astype(jnp.int32)
        row_o[s] = turned[8 * s : 8 * s + 1, :]


def index_requests(ids, rows, owners, slots):
    count, n = ids.shape
    return pl.pallas_call(
        functools.partial(index_kernel, rows=rows, slots=slots),
        grid=(1,),
        in_specs=[whole((count, n))],
        out_specs=[whole((owners, slots)), whole((count + 1, n, 1)), whole((count + 1, 1, n))],
        out_shape=[
            struct((owners, slots), jnp.int32),
            struct((count + 1, n, 1), jnp.int32),
            struct((count + 1, 1, n), jnp.int32),
        ],
        compiler_params=params(),
        cost_estimate=cost(0, 1e6),
        name="index_requests",
    )(ids)


def gather_kernel(fetch, table, out, acc, *, rows):
    step = pl.program_id(0)
    last = pl.num_programs(0) - 1
    blk = table.shape[0]
    ids = lax.broadcasted_iota(jnp.int32, (1, blk), 1) + step * blk
    hot = jnp.where(ids == fetch[...], 1.0, 0.0).astype(LOW)

    def add(block):
        part = nn(hot, block)

        @pl.when(step == 0)
        def _():
            acc[...] = part

        @pl.when(step > 0)
        def _():
            acc[...] += part

    @pl.when(step < last)
    def _():
        add(table[...])

    @pl.when(step == last)
    def _():
        ids_col = lax.broadcasted_iota(jnp.int32, (blk, 1), 0) + step * blk
        add(jnp.where(ids_col < rows, table[...], jnp.zeros((), LOW)))
        out[...] = acc[...].astype(LOW)


def gather_rows(fetch, table, blk=1024):
    slots = fetch.shape[0]
    rows, d = table.shape
    return pl.pallas_call(
        functools.partial(gather_kernel, rows=rows),
        grid=(pl.cdiv(rows, blk),),
        in_specs=[whole((slots, 1)), pl.BlockSpec((blk, d), lambda i: (i, 0))],
        out_specs=whole((slots, d)),
        out_shape=struct((slots, d), LOW),
        scratch_shapes=[pltpu.VMEM((slots, d), F32)],
        compiler_params=params(),
        cost_estimate=cost(2 * slots * rows * d, 8e6),
        name="gather_rows",
    )(fetch, table)


def embed_kernel(place, slot, replies, pos, o0, o1, o2, o3):
    ids = lax.broadcasted_iota(jnp.int32, (1, replies.shape[0]), 1)
    for m, out in enumerate((o0, o1, o2, o3)):
        sent = (place[0] + m) % 4
        hot = jnp.where(ids == slot[sent], 1.0, 0.0).astype(LOW)
        live = jnp.where(sent < 3, 1.0, 0.0)
        out[...] = ((nn(hot, replies[...]) + pos[...].astype(F32)) * live).astype(LOW)


def embed_parts(place, slot, replies, pos):
    slots, d = replies.shape
    n = pos.shape[0]
    out = pl.BlockSpec((n, d), lambda i, p: (0, 0))
    return pl.pallas_call(
        embed_kernel,
        grid_spec=prefetch(
            1,
            (1,),
            [whole((4, n, 1)), whole((slots, d)), whole((n, d))],
            [out] * 4,
        ),
        out_shape=[struct((n, d), LOW)] * 4,
        compiler_params=params(),
        cost_estimate=cost(2 * slots * 4 * n * d, 3e6),
        name="embed_parts",
    )(place, slot, replies, pos)


def outgoing_kernel(place, slot, p0, p1, p2, p3, out):
    ids = lax.broadcasted_iota(jnp.int32, (out.shape[0], 1), 0)
    total = 0.0
    for m, part in enumerate((p0, p1, p2, p3)):
        sent = (place[0] + m) % 4
        hot = jnp.where(ids == slot[sent], 1.0, 0.0).astype(LOW)
        total = total + nn(hot, part[...])
    out[...] = total.astype(LOW)


def outgoing_rows(place, slot, parts, slots):
    n = slot.shape[2]
    d = parts[0].shape[1]
    return pl.pallas_call(
        outgoing_kernel,
        grid_spec=prefetch(
            1, (1,), [whole((4, 1, n))] + [whole((n, d))] * 4, whole((slots, d))
        ),
        out_shape=struct((slots, d), LOW),
        compiler_params=params(),
        cost_estimate=cost(2 * slots * 4 * n * d, 3e6),
        name="outgoing_rows",
    )(place, slot, *parts)


def table_kernel(fetch, incoming, out):
    blk = out.shape[0]
    ids = lax.broadcasted_iota(jnp.int32, (blk, 1), 0) + pl.program_id(0) * blk
    out[...] = nn(jnp.where(ids == fetch[...], 1.0, 0.0).astype(LOW), incoming[...])


def table_grad(fetch, incoming, rows, blk=1024):
    slots, d = incoming.shape
    return pl.pallas_call(
        table_kernel,
        grid=(pl.cdiv(rows, blk),),
        in_specs=[whole((1, slots)), whole((slots, d))],
        out_specs=pl.BlockSpec((blk, d), lambda i: (i, 0)),
        out_shape=struct((rows, d), F32),
        compiler_params=params(),
        cost_estimate=cost(2 * slots * rows * d, 13e6),
        name="table_gradient",
    )(fetch, incoming)


def unpermute_kernel(place, p0, p1, p2, p3, out):
    for m, part in enumerate((p0, p1, p2, p3)):
        sent = (place[0] + m) % 4

        @pl.when(sent < 3)
        def _():
            out[sent] = part[...]


def unpermute(place, parts, n):
    d = parts[0].shape[1]
    return pl.pallas_call(
        unpermute_kernel,
        grid_spec=prefetch(1, (1,), [whole((n, d))] * 4, whole((3, n, d))),
        out_shape=struct((3, n, d), parts[0].dtype),
        compiler_params=params(),
        cost_estimate=cost(0, 2e6),
        name="unpermute",
    )(place, *parts)


def ff_send_kernel(which, left, right, out):
    out[0] = tn(left[0], right[0, 0]).astype(LOW)


def ff_specs(s, d):
    return [
        pl.BlockSpec((1, s, d), lambda f, w: (w[0], 0, 0)),
        pl.BlockSpec((1, 1, s, d), lambda f, w: (w[0], f, 0, 0)),
    ]


def ff_send(which, left, right):
    _, blocks, s, d = right.shape
    return pl.pallas_call(
        ff_send_kernel,
        grid_spec=prefetch(
            1, (blocks,), ff_specs(s, d), pl.BlockSpec((1, d, d), lambda f, w: (f, 0, 0))
        ),
        out_shape=struct((blocks, d, d), LOW),
        compiler_params=params(),
        cost_estimate=cost(2 * blocks * s * d * d, 9e6),
        name="ff_send",
    )(which, left, right)


def ff_keep_kernel(place, left, right, got, o0, o1, o2, o3, acc):
    f = pl.program_id(0)
    total = tn(left[0], right[0, 0]) + got[0].astype(F32)
    acc[f] = total.astype(LOW).reshape(acc.shape[1:])

    @pl.when(f == pl.num_programs(0) - 1)
    def _():
        for m, out in enumerate((o0, o1, o2, o3)):
            index = (place[1] + m) % 4

            @pl.when(place[0] == 0)
            def _():
                for z in range(4):
                    out[z] = acc[z, index]

            @pl.when(place[0] == 1)
            def _():
                out[...] = acc[index]


def ff_keep(place, left, right, got):
    _, blocks, s, d = right.shape
    shape = (4, d // 4, d)
    return pl.pallas_call(
        ff_keep_kernel,
        grid_spec=prefetch(
            1,
            (blocks,),
            ff_specs(s, d) + [pl.BlockSpec((1, d, d), lambda f, w: (f, 0, 0))],
            [whole(shape)] * 4,
            [pltpu.VMEM((blocks,) + shape, LOW)],
        ),
        out_shape=[struct(shape, LOW)] * 4,
        compiler_params=params(),
        cost_estimate=cost(2 * blocks * s * d * d, 14e6),
        name="ff_keep",
    )(place, left, right, got)


def core_add_kernel(place, own, got, o0, o1, o2, o3):
    rows = o0.shape[1]
    for m, out in enumerate((o0, o1, o2, o3)):
        at = pl.ds(pl.multiple_of((place[0] + m) % 4 * rows, rows), rows)
        out[...] = (own[:, at, :].astype(F32) + got[:, at, :].astype(F32)).astype(LOW)


def core_add(place, own, got):
    out = (4, own.shape[1] // 4, own.shape[2])
    return pl.pallas_call(
        core_add_kernel,
        grid_spec=prefetch(1, (1,), [whole(own.shape)] * 2, [whole(out)] * 4),
        out_shape=[struct(out, LOW)] * 4,
        compiler_params=params(),
        cost_estimate=cost(0, 9e6),
        name="core_add",
    )(place, own, got)


def add4(a, b, c, d):
    return a[...].astype(F32) + b[...].astype(F32) + c[...].astype(F32) + d[...].astype(F32)


def ring_add_kernel(place, p0, p1, p2, p3, o0, o1, o2, o3, acc):
    acc[...] = add4(p0, p1, p2, p3)
    rows = o0.shape[1]
    for m, out in enumerate((o0, o1, o2, o3)):
        at = pl.ds(pl.multiple_of((place[0] + m) % 4 * rows, rows), rows)
        out[...] = acc[:, at, :].astype(LOW)


def ring_add(place, parts):
    shape = parts[0].shape
    out = (4, shape[1] // 4, shape[2])
    return pl.pallas_call(
        ring_add_kernel,
        grid_spec=prefetch(
            1, (1,), [whole(shape)] * 4, [whole(out)] * 4, [pltpu.VMEM(shape, F32)]
        ),
        out_shape=[struct(out, LOW)] * 4,
        compiler_params=params(),
        cost_estimate=cost(0, 6e6),
        name="ring_add",
    )(place, *parts)


def join_kernel(place, a0, a1, a2, a3, b0, b1, b2, b3, o0, o1, o2, o3, acc):
    acc[:, 0:48, :] = add4(a0, a1, a2, a3)
    acc[:, 48:80, :] = add4(b0, b1, b2, b3)
    for m, out in enumerate((o0, o1, o2, o3)):
        out[...] = acc[(place[0] + m) % 4].astype(LOW)


def join(place, first, second):
    d = first[0].shape[2]
    return pl.pallas_call(
        join_kernel,
        grid_spec=prefetch(
            1,
            (1,),
            [whole(first[0].shape)] * 4 + [whole(second[0].shape)] * 4,
            [whole((80, d))] * 4,
            [pltpu.VMEM((4, 80, d), F32)],
        ),
        out_shape=[struct((80, d), LOW)] * 4,
        compiler_params=params(),
        cost_estimate=cost(0, 4e6),
        name="join",
    )(place, *first, *second)


def piece_kernel(f0, f1, f2, f3, r0, r1, r2, r3, out):
    pool = [part[...].astype(F32)[0:2] for part in (r0, r1, r2, r3)]
    pool.append(jnp.zeros((8, out.shape[1]), F32))
    out[...] = jnp.concatenate([add4(f0, f1, f2, f3)] + pool, axis=0).astype(LOW)


def piece_rows(parts, pool):
    d = parts[0].shape[1]
    return pl.pallas_call(
        piece_kernel,
        grid=(1,),
        in_specs=[whole(p.shape) for p in parts]
        + [pl.BlockSpec((16, d), lambda i: (8, 0)) for p in pool],
        out_specs=whole((96, d)),
        out_shape=struct((96, d), LOW),
        compiler_params=params(),
        cost_estimate=cost(0, 1e6),
        name="piece_rows",
    )(*parts, *pool)


def order_kernel(place, p0, p1, p2, p3, out):
    for m, part in enumerate((p0, p1, p2, p3)):
        out[(place[0] + 4 - m) % 4] = part[...]


def order(place, parts):
    shape = parts[0].shape
    return pl.pallas_call(
        order_kernel,
        grid_spec=prefetch(1, (1,), [whole(shape)] * 4, whole((4,) + shape)),
        out_shape=struct((4,) + shape, LOW),
        compiler_params=params(),
        cost_estimate=cost(0, 3e6),
        name="order",
    )(place, *parts)


def finish_kernel(
    place, own, got, outer_o, inner_o, q_o, k_o, v_o, out_o, pos_o, vec_o, pw_o, pb_o, acc
):
    d = outer_o.shape[0]

    def fill(zero, one):
        pool = []
        for i in range(4):
            for k in range(4):
                at = 96 * k
                r = 192 * i + 48 * k
                acc[r : r + 48, :] = zero[i, at : at + 48, :].astype(F32)
                cols = slice(d * i, d * i + d)
                inner_o[48 * k : 48 * k + 48, cols] = one[i, at : at + 48, :].astype(F32)
                r = 128 * i + 32 * k
                first = zero[i, at + 48 : at + 80, :].astype(F32)
                second = one[i, at + 48 : at + 80, :].astype(F32)
                if r < 192:
                    q_o[r : r + 32, :] = first
                    v_o[r : r + 32, :] = second
                elif r < 384:
                    k_o[r - 192 : r - 160, :] = first
                    out_o[r - 192 : r - 160, :] = second
                else:
                    pos_o[r - 384 : r - 352, :] = first
                    if r == 384:
                        vec_o[...] = second[0:16]
                pool.append(zero[i, at + 80 : at + 96, :].astype(F32)[0:8])
                pool.append(one[i, at + 80 : at + 96, :].astype(F32)[0:8])
        outer_o[...] = acc[...].T
        pool = jnp.concatenate(pool, axis=0)
        even = lax.broadcasted_iota(jnp.int32, (pool.shape[0], 1), 0) % 2 == 0
        below = jnp.concatenate([pool[1:], pool[:1]], axis=0)
        acc[...] = tn(jnp.where(even, pool, 0.0).astype(LOW), below.astype(LOW))
        pb_o[...] = jnp.sum(jnp.where(even, 0.0, pool), axis=0, keepdims=True)

    @pl.when(place[0] == 0)
    def _():
        fill(own, got)

    @pl.when(place[0] == 1)
    def _():
        fill(got, own)

    pw_o[...] = acc[pl.ds(pl.multiple_of(place[1] * (d // 4), d // 4), d // 4), :]


def finish(place, own, got):
    d = own.shape[2]
    share = d // 4
    shapes = [(d, d), (share, 4 * d)] + [(share, d)] * 4 + [(128, d), (16, d), (share, d), (1, d)]
    return pl.pallas_call(
        finish_kernel,
        grid_spec=prefetch(
            1,
            (1,),
            [whole(own.shape)] * 2,
            [whole(s) for s in shapes],
            [pltpu.VMEM((d, d), F32)],
        ),
        out_shape=[struct(s, F32) for s in shapes],
        compiler_params=params(),
        cost_estimate=cost(0, 14e6),
        name="finish",
    )(place, own, got)


def pooled_kernel(place, p0, p1, p2, p3, out):
    for m, part in enumerate((p0, p1, p2, p3)):
        two = part[...].astype(F32)
        row = two[2:3] + two[3:4]
        out[(place[0] + m) % 4] = pltpu.roll(
            jnp.broadcast_to(row, (8, row.shape[1])), row.shape[1] - 192 * place[0], 1
        )


def pooled_rows(place, parts):
    d = parts[0].shape[1]
    below = pl.BlockSpec((16, d), lambda i, p: (8, 0))
    return pl.pallas_call(
        pooled_kernel,
        grid_spec=prefetch(1, (1,), [below] * 4, whole((4, 8, d))),
        out_shape=struct((4, 8, d), F32),
        compiler_params=params(),
        name="pooled_rows",
    )(place, *parts)


def shift_pairs(step, axes):
    pairs = []
    for y in range(4):
        for x in range(4):
            for c in range(2):
                to = (y, (x + step) % 4) if axes[c] == "x" else ((y + step) % 4, x)
                pairs.append(((y * 4 + x) * 2 + c, (to[0] * 4 + to[1]) * 2 + c))
    return pairs


def shift_first(array, step):
    return lax.ppermute(array, "batch", shift_pairs(step, "xy"))


def shift_second(array, step):
    return lax.ppermute(array, "batch", shift_pairs(step, "yx"))


def shift_z(array, step):
    return lax.ppermute(array, "seq", [(z, (z + step) % 4) for z in range(4)])


def swap_core(array):
    return lax.ppermute(array, "batch", [(i, i ^ 1) for i in range(32)])


def ring_send(parts, shift):
    return [parts[0], shift(parts[1], 1), shift(parts[2], 2), shift(parts[3], 3)]


def to_sentence(parts):
    out = [parts[0]]
    for step in (1, 2, 3):
        pairs = [(z, (z + step) % 4) for z in range(4) if (z + step) % 4 < 3]
        out.append(lax.ppermute(parts[step], "seq", pairs))
    return out


def from_sentence(parts):
    out = [parts[0]]
    for step in (1, 2, 3):
        pairs = [((z + step) % 4, z) for z in range(4) if (z + step) % 4 < 3]
        out.append(lax.ppermute(parts[step], "seq", pairs))
    return out


def tie(array, *after):
    return lax.optimization_barrier((array,) + after)[0]


def per_device(
    token_ids,
    lengths,
    word_table,
    positions,
    query_weight,
    key_weight,
    value_weight,
    query_bias,
    value_bias,
    output_weight,
    output_bias,
    first_gain,
    first_shift,
    inner_weight,
    inner_bias,
    outer_weight,
    outer_bias,
    second_gain,
    second_shift,
    pooler_weight,
    pooler_bias,
    out_grad,
    pooled_grad,
):
    num_sent, local_len = token_ids.shape
    table_rows, width = word_table.shape
    all_count = lax.axis_size("seq") * lax.axis_size("batch")
    z = lax.axis_index("seq")
    batch_place = lax.axis_index("batch")
    core = batch_place % 2
    x = (batch_place // 2) % 4
    y = batch_place // 8

    first = jnp.where(core == 0, x, y)
    second = jnp.where(core == 0, y, x)

    def scalars(*values):
        return jnp.stack([jnp.asarray(v, jnp.int32) for v in values])

    slots = 2 * num_sent * local_len // all_count
    all_slots = slots * all_count
    requests, slot_cols, slot_rows = index_requests(token_ids, table_rows, all_count, slots)
    arrived = lax.all_to_all(requests, ("batch", "seq"), split_axis=0, concat_axis=0, tiled=True)
    fetch = arrived.reshape(-1)
    found = gather_rows(fetch[:, None], word_table)
    replies = lax.all_to_all(
        found.reshape(all_count, slots, width),
        ("batch", "seq"),
        split_axis=0,
        concat_axis=0,
        tiled=True,
    ).reshape(all_slots, width)
    live = (z < 3).astype(jnp.int32)
    sentence = jnp.minimum(z, 2)

    def row(vector):
        return vector.reshape(1, -1)

    vectors = (
        query_bias,
        value_bias,
        output_bias,
        first_gain,
        first_shift,
        inner_bias,
        outer_bias,
        second_gain,
        second_shift,
        pooler_bias,
    )
    block_of = (z - jnp.arange(4, dtype=jnp.int32)) % 4
    place_of = block_of[:, None] * local_len + jnp.arange(local_len, dtype=jnp.int32)[None, :]
    live_keys = (place_of.reshape(-1, 1) < lengths[sentence]).astype(F32)

    high = pooled_grad.astype(LOW)
    terms = jnp.stack([high, (pooled_grad - high.astype(F32)).astype(LOW)], axis=1)
    terms = jnp.pad(terms, ((0, 0), (0, 14), (0, width - terms.shape[2])))
    cotangents = jnp.concatenate([out_grad, terms], axis=1)
    early = [live_keys] + [row(v) for v in vectors]
    cotangents, *early = lax.optimization_barrier([cotangents] + early)
    live_keys, q_bias, v_bias, o_bias, gain1, shift1, in_bias, out_bias, gain2, shift2, pool_bias = early
    ups = [
        lax.dynamic_index_in_dim(cotangents, jnp.minimum((z + m) % 4, 2), 0, keepdims=False)
        for m in range(4)
    ]
    ups = to_sentence([jnp.where(z < 3, ups[0], jnp.zeros((), LOW))] + ups[1:])
    replies, *ups = lax.optimization_barrier([replies] + ups)
    embeds = to_sentence(embed_parts(scalars(z), slot_cols, replies, positions))

    embed, query, key, value, expo, inverse, mixed_t, mixed = attn_fwd(
        embeds, query_weight, key_weight, value_weight, q_bias, v_bias, live_keys
    )
    (
        left,
        right,
        *result,
        pool,
        attention_low,
        first_back,
        vec1,
        vec2,
        inner_bias_grad,
    ) = feed_forward(
        scalars(sentence * local_len, live, z),
        mixed,
        output_weight,
        o_bias,
        embed,
        gain1,
        shift1,
        inner_weight,
        in_bias,
        outer_weight,
        out_bias,
        gain2,
        shift2,
        pooler_weight,
        pool_bias,
        ups,
    )

    ff_other = ff_send(scalars(1 - core), left, right)
    ff_parts = ff_keep(scalars(core, first), left, right, swap_core(ff_other))
    attention_low = tie(attention_low, ff_parts[0])
    ff_parts = ring_send(ff_parts, shift_first)
    *embed_grad, rest_other, rest_own = attn_bwd(
        scalars(z, core),
        attention_low,
        output_weight,
        query,
        key,
        value,
        expo,
        inverse,
        mixed_t,
        query_weight,
        key_weight,
        value_weight,
        embed,
        first_back,
        mixed,
        pool,
        vec1,
        vec2,
        inner_bias_grad,
    )
    embed_grad, rest_other, rest_own, ff_parts = lax.optimization_barrier(
        (embed_grad, rest_other, rest_own, ff_parts)
    )

    returned = from_sentence(embed_grad)
    rest_parts = core_add(scalars(first), rest_own, swap_core(rest_other))
    ff_parts[0] = tie(ff_parts[0], rest_parts[0])
    rest_parts = ring_send(rest_parts, shift_first)
    ff_parts = ring_add(scalars(second), ff_parts)
    returned[0] = tie(returned[0], ff_parts[0])
    outgoing = outgoing_rows(scalars(z), slot_rows, returned, all_slots)
    ff_parts = ring_send(ff_parts, shift_second)
    incoming = lax.all_to_all(
        outgoing.reshape(all_count, slots, width),
        ("batch", "seq"),
        split_axis=0,
        concat_axis=0,
        tiled=True,
    ).reshape(all_slots, width)
    rest_parts[0] = tie(rest_parts[0], outgoing)
    rest_parts = ring_send(ring_add(scalars(second), rest_parts), shift_second)
    rest_parts[0] = tie(rest_parts[0], incoming)
    parts = ring_send(join(scalars(z), ff_parts, rest_parts), shift_z)
    piece = piece_rows(parts, returned)
    incoming = tie(incoming, piece)
    pieces = [piece] + [shift_second(piece, m) for m in (1, 2, 3)]
    grad_table = table_grad(fetch[None, :], incoming, table_rows)
    pieces[0] = tie(pieces[0], grad_table)
    block = order(scalars(second), pieces).reshape(-1, width)
    result[0] = tie(result[0], block)
    blocks = [block] + [shift_first(block, m) for m in (1, 2, 3)]
    result = from_sentence(result)
    pooled = pooled_rows(scalars(z), [tie(returned[0], block)] + returned[1:])
    pooled = pooled[:num_sent, 0, : width // 4]
    blocks[0] = tie(blocks[0], pooled)
    whole_own = order(scalars(first), blocks)
    whole_other = swap_core(whole_own)
    result[0] = tie(result[0], whole_own)
    hidden_out = unpermute(scalars(z), result, local_len)
    (
        grad_outer,
        grad_inner,
        grad_query,
        grad_key,
        grad_value,
        grad_output,
        grad_positions,
        vectors,
        grad_pooler,
        pooler_bias_grad,
    ) = finish(scalars(core, z), tie(whole_own, hidden_out), whole_other)

    share = width // 4
    mine = lax.dynamic_slice_in_dim(vectors[:8], z * share, share, 1)
    ff = inner_weight.shape[1]
    inner_bias_sum = lax.dynamic_slice_in_dim(vectors[8:12].reshape(-1), z * ff // 4, ff // 4, 0)
    pooler_bias_sum = lax.dynamic_slice_in_dim(pooler_bias_grad[0], z * share, share, 0)
    return (
        hidden_out,
        pooled,
        grad_table,
        grad_positions,
        grad_query,
        grad_key,
        grad_value,
        mine[0],
        mine[1],
        grad_output,
        mine[2],
        mine[3],
        mine[4],
        grad_inner,
        inner_bias_sum,
        grad_outer,
        mine[5],
        mine[6],
        mine[7],
        grad_pooler,
        pooler_bias_sum,
    )


def solution(mesh):
    in_specs = (
        P("batch", "seq"),
        P("batch"),
        P(("batch", "seq"), None),
        P("seq", None),
        P(),
        P(),
        P(),
        P(),
        P(),
        P(),
        P(),
        P(),
        P(),
        P(),
        P(),
        P(),
        P(),
        P(),
        P(),
        P(),
        P(),
        P("batch", "seq", None),
        P("batch", "seq"),
    )
    out_specs = (
        P("batch", "seq", None),
        P("batch", "seq"),
        P(("batch", "seq"), None),
        P("seq", None),
        P("seq", None),
        P("seq", None),
        P("seq", None),
        P("seq"),
        P("seq"),
        P("seq", None),
        P("seq"),
        P("seq"),
        P("seq"),
        P("seq", None),
        P("seq"),
        P("seq", None),
        P("seq"),
        P("seq"),
        P("seq"),
        P("seq", None),
        P("seq"),
    )
    return jax.shard_map(
        per_device, mesh=mesh, in_specs=in_specs, out_specs=out_specs, check_vma=False
    )
```

profile of v0, /device:TPU:1, one launch (start us, length us, event | category | flops | bytes accessed | tf_op | source)
XLA Modules:
  0.0 363.3 jit_solution(10109822862240397958)
XLA Ops:
  3.0 21.1 %all_to_all.19 = s32[128,1,6]{2,1,0:T(1,128)S(1)} all-to-all(s32[128,1,6]{2,1,0:T(1,128)} %bitcast.44), channel_id=1, replica_groups=mesh['batch'=32,'seq'=4] {'batch','seq'}, dimensions={0} | all-to-all | bytes 6144 | tf_op jit(solution)/shard_map/all_to_all | solution.py:1010
  26.3 9.8 %gather_rows.1 = bf16[768,768]{1,0:T(8,128)(2,1)} custom-call(s32[768,1]{1,0:T(8,128)} %broadcast_in_dim_reshape.8.fetch, bf16[3912,768]{1,0:T(8,128)(2,1)} %table.1), custom_call_target="tpu_custom_call" | custom-call | flops 92295656 | bytes 160000 | tf_op jit(solution)/shard_map/gather_rows/pallas_call | solution.py:549
  36.0 3.2 reshape.152
  39.4 4.3 %all-to-all-start.1 = ((bf16[128,6,768]{2,1,0:T(8,128)(2,1)}), bf16[128,6,768]{2,1,0:T(8,128)(2,1)S(1)}, u32[]{:S(2)}, u32[]{:S(2)}) async-start(bf16[128,6,768]{2,1,0:T(8,128)(2,1)} %reshape.152), calls=%async_computation.1 | async-start | bytes 3145728 | tf_op jit(solution)/shard_map/all_to_all | solution.py:1013
  53.2 5.8 %collective-permute-start.1 = (bf16[144,768]{1,0:T(8,128)(2,1)S(1)}, bf16[144,768]{1,0:T(8,128)(2,1)S(1)}, u32[]{:S(2)}, u32[]{:S(2)}) collective-permute-start(bf16[144,768]{1,0:T(8,128)(2,1)S(1)} %get-tuple-element.226), channel_id=1, source_target_pairs={{0,2},{2,0},{3,1},{4,6},{6,4},{7,5},{8,10},{10,8},{11,9},{12,14},{... | collective-permute-start | bytes 663560 | tf_op jit(solution)/shard_map/ppermute | solution.py:951
  60.9 7.7 %all-to-all-done.1 = bf16[128,6,768]{2,1,0:T(8,128)(2,1)S(1)} async-done(((bf16[128,6,768]{2,1,0:T(8,128)(2,1)}), bf16[128,6,768]{2,1,0:T(8,128)(2,1)S(1)}, u32[]{:S(2)}, u32[]{:S(2)}) %all-to-all-start.1) | async-done | bytes 1179680 | tf_op jit(solution)/shard_map/all_to_all | solution.py:1013
  70.7 4.9 %collective-permute-done.u1 = bf16[144,768]{1,0:T(8,128)(2,1)S(1)} collective-permute-done((bf16[144,768]{1,0:T(8,128)(2,1)S(1)}, bf16[144,768]{1,0:T(8,128)(2,1)S(1)}, u32[]{:S(2)}, u32[]{:S(2)}) %collective-permute-start) | collective-permute-done | bytes 221216 | tf_op jit(solution)/shard_map/ppermute | solution.py:951
  85.5 6.7 %collective-permute-done.3.x1 = bf16[128,768]{1,0:T(8,128)(2,1)S(1)} collective-permute-done((bf16[128,768]{1,0:T(8,128)(2,1)}, bf16[128,768]{1,0:T(8,128)(2,1)S(1)}, u32[]{:S(2)}, u32[]{:S(2)}) %collective-permute-start.3) | collective-permute-done | bytes 196640 | tf_op jit(solution)/shard_map/ppermute | solution.py:951
  93.0 12.0 %attention_forward.1 = (bf16[512,768]{1,0:T(8,128)(2,1)}, bf16[512,768]{1,0:T(8,128)(2,1)}, bf16[512,768]{1,0:T(8,128)(2,1)}, bf16[512,768]{1,0:T(8,128)(2,1)}, ...) custom-call(bf16[128,768]{1,0:T(8,128)(2,1)} %get-tuple-element.127., ...), custom_call_target="tpu_custom_call" | custom-call | flops 100663296 | bytes 320000 | tf_op jit(solution)/shard_map/attention_forward/pallas_call | solution.py:94
  105.0 23.0 %feed_forward.1 = (bf16[2,512,768]{2,1,0:T(8,128)(2,1)}, bf16[2,4,512,768]{3,2,1,0:T(8,128)(2,1)}, bf16[128,768]{1,0:T(8,128)(2,1)}, bf16[128,768]{1,0:T(8,128)(...) custom-call(s32[3]{0:T(128)} %pad_add_fusion.row0, ...), custom_call_target="tpu_custom_call" | custom-call | flops 205353120 | bytes 600000 | tf_op jit(solution)/shard_map/feed_forward/pallas_call | solution.py:410
  128.1 6.5 %ff_send.1 = bf16[4,768,768]{2,1,0:T(8,128)(2,1)} custom-call(s32[1]{0:T(128)} %bitcast.17.which, bf16[2,512,768]{2,1,0:T(8,128)(2,1)} %get-tuple-element.150.left, bf16[2,4,512,768]{3,2,1,0:T(8,128)(2,1)} %get-tuple-element.151.right), custom_call_target="tpu_custom_call" | custom-call | flops 48318384 | bytes 180000 | tf_op jit(solution)/shard_map/ff_send/pallas_call | solution.py:669
  136.8 7.3 %collective-permute-done.6.got = bf16[4,768,768]{2,1,0:T(8,128)(2,1)} collective-permute-done((bf16[4,768,768]{2,1,0:T(8,128)(2,1)}, bf16[4,768,768]{2,1,0:T(8,128)(2,1)}, u32[]{:S(2)}, u32[]{:S(2)}) %collective-permute-start.6) | collective-permute-done | bytes 4718624 | tf_op jit(solution)/shard_map/ppermute | solution.py:940
  144.1 9.1 %ff_keep.1 = (bf16[4,192,768]{2,1,0:T(8,128)(2,1)}, bf16[4,192,768]{2,1,0:T(8,128)(2,1)}, bf16[4,192,768]{2,1,0:T(8,128)(2,1)}, bf16[4,192,768]{2,1,0:T(8,128)(2,1)}) custom-call(s32[2]{0:T(128)} %pad_add_fusion.2.place, bf16[2,512,768]{2,1,0:T(8,128)(2,1)} %get-tuple-element.150.left, bf16[2,4,512,768]{3,2,1,0:T(8,128)(2,1)} %get-tuple-element.151.right, ...), custom_call_target="tpu_custom_call" | custom-call | flops 48318384 | bytes 280000 | tf_op jit(solution)/shard_map/ff_keep/pallas_call | solution.py:704
  157.4 24.6 %attention_backward.1 = (bf16[144,768]{1,0:T(8,128)(2,1)}, bf16[144,768]{1,0:T(8,128)(2,1)}, bf16[144,768]{1,0:T(8,128)(2,1)}, bf16[144,768]{1,0:T(8,128)(2,1)},...) custom-call(s32[2]{0:T(128)} %pad_add_fusion.1.place, bf16[512,768]{1,0:T(8,128)(2,1)} %get-tuple-element.153.al, ...), custom_call_target="tpu_custom_call" | custom-call | flops 213406192 | bytes 560000 | tf_op jit(solution)/shard_map/attention_backward/pallas_call | solution.py:242
  184.9 3.1 collective-permute-start.14
  188.0 4.9 %collective-permute-start.15 = (bf16[144,768]{1,0:T(8,128)(2,1)}, bf16[144,768]{1,0:T(8,128)(2,1)}, u32[]{:S(2)}, u32[]{:S(2)}) collective-permute-start(bf16[144,768]{1,0:T(8,128)(2,1)} %get-tuple-element.190), channel_id=1, source_target_pairs={{2,0},{0,2},{1,3},{6,4},{4,6},{5,7},{10,8},{8,10},{9,11},{14,12},{... | collective-permute-start | bytes 663560 | tf_op jit(solution)/shard_map/ppermute | solution.py:959
  196.8 5.1 %core_add.1 = (bf16[4,128,768]{2,1,0:T(8,128)(2,1)}, bf16[4,128,768]{2,1,0:T(8,128)(2,1)}, bf16[4,128,768]{2,1,0:T(8,128)(2,1)}, bf16[4,128,768]{2,1,0:T(8,128)(2,1)}) custom-call(s32[1]{0:T(128)} %bitcast.16.place, bf16[4,512,768]{2,1,0:T(8,128)(2,1)} %get-tuple-element.175.own, bf16[4,512,768]{2,1,0:T(8,128)(2,1)} %copy-done), custom_call_target="tpu_custom_call" | custom-call | bytes 180000 | tf_op jit(solution)/shard_map/core_add/pallas_call | solution.py:729
  201.9 4.4 %ring_add.2 = (bf16[4,48,768]{2,1,0:T(8,128)(2,1)}, bf16[4,48,768]{2,1,0:T(8,128)(2,1)}, bf16[4,48,768]{2,1,0:T(8,128)(2,1)}, bf16[4,48,768]{2,1,0:T(8,128)(2,1)}) custom-call(s32[1]{0:T(128)} %bitcast.14.place, bf16[4,192,768]{2,1,0:T(8,128)(2,1)} %get-tuple-element.178.p0, bf16[4,192,768]{2,1,0:T(8,128)(2,1)} %copy-done.3, bf16[4,192,768]{2,1,0:T(8,128)(2,1)} %copy-done.4, ...), custom_call_target="tpu_custom_call" | custom-call | bytes 120000 | tf_op jit(solution)/shard_map/ring_add/pallas_call | solution.py:754
  207.0 3.6 outgoing_rows.1
  210.6 3.2 reshape.165
  213.8 5.1 %all-to-all-start.2 = ((bf16[128,6,768]{2,1,0:T(8,128)(2,1)}), bf16[128,6,768]{2,1,0:T(8,128)(2,1)S(1)}, u32[]{:S(2)}, u32[]{:S(2)}) async-start(bf16[128,6,768]{2,1,0:T(8,128)(2,1)} %reshape.165), calls=%async_computation.2 | async-start | bytes 3145728 | tf_op jit(solution)/shard_map/all_to_all | solution.py:1126
  227.5 26.1 %collective-permute-done.17.p1 = bf16[4,128,768]{2,1,0:T(8,128)(2,1)S(1)} collective-permute-done((bf16[4,128,768]{2,1,0:T(8,128)(2,1)}, bf16[4,128,768]{2,1,0:T(8,128)(2,1)S(1)}, u32[]{:S(2)}, u32[]{:S(2)}) %collective-permute-start.17) | collective-permute-done | bytes 786464 | tf_op jit(solution)/shard_map/ppermute | solution.py:928
  256.1 6.3 %collective-permute-done.18.p2 = bf16[4,128,768]{2,1,0:T(8,128)(2,1)S(1)} collective-permute-done((bf16[4,128,768]{2,1,0:T(8,128)(2,1)}, bf16[4,128,768]{2,1,0:T(8,128)(2,1)S(1)}, u32[]{:S(2)}, u32[]{:S(2)}) %collective-permute-start.18) | collective-permute-done | bytes 786464 | tf_op jit(solution)/shard_map/ppermute | solution.py:928
  264.2 3.4 ring_add.3
  296.9 8.6 %table_gradient.1 = f32[3912,768]{1,0:T(8,128)} custom-call(s32[1,768]{1,0:T(1,128)} %broadcast_in_dim_reshape.7.fetch, bf16[768,768]{1,0:T(8,128)(2,1)} %reshape.166.incoming), custom_call_target="tpu_custom_call" | custom-call | flops 92295656 | bytes 260000 | tf_op jit(solution)/shard_map/table_gradient/pallas_call | solution.py:623
  313.2 4.9 %collective-permute-done.31.p3 = bf16[384,768]{1,0:T(8,128)(2,1)S(1)} collective-permute-done((bf16[384,768]{1,0:T(8,128)(2,1)}, bf16[384,768]{1,0:T(8,128)(2,1)S(1)}, u32[]{:S(2)}, u32[]{:S(2)}) %collective-permute-start.31) | collective-permute-done | bytes 589856 | tf_op jit(solution)/shard_map/ppermute | solution.py:928
  319.7 6.3 %collective-permute-done.29.p1 = bf16[384,768]{1,0:T(8,128)(2,1)S(1)} collective-permute-done((bf16[384,768]{1,0:T(8,128)(2,1)}, bf16[384,768]{1,0:T(8,128)(2,1)S(1)}, u32[]{:S(2)}, u32[]{:S(2)}) %collective-permute-start.29) | collective-permute-done | bytes 589856 | tf_op jit(solution)/shard_map/ppermute | solution.py:928
  326.8 3.1 order.3.own
  329.9 3.2 collective-permute-start.35
  333.1 4.0 %collective-permute-start.32 = (bf16[128,768]{1,0:T(8,128)(2,1)S(1)}, bf16[128,768]{1,0:T(8,128)(2,1)S(1)}, u32[]{:S(2)}, u32[]{:S(2)}) collective-permute-start(bf16[128,768]{1,0:T(8,128)(2,1)S(1)} %copy-done.48), channel_id=1, source_target_pairs={{1,0},{2,1},{0,3},{5,4},{6,5},{4,7},{9,8},{10,9},{8,11},{13,12},{1... | collective-permute-start | bytes 589832 | tf_op jit(solution)/shard_map/ppermute | solution.py:959
  341.7 3.8 %collective-permute-done.32.p1 = bf16[128,768]{1,0:T(8,128)(2,1)S(1)} collective-permute-done((bf16[128,768]{1,0:T(8,128)(2,1)S(1)}, bf16[128,768]{1,0:T(8,128)(2,1)S(1)}, u32[]{:S(2)}, u32[]{:S(2)}) %collective-permute-start.32) | collective-permute-done | bytes 196640 | tf_op jit(solution)/shard_map/ppermute | solution.py:959
  352.2 7.4 %finish.1 = (f32[768,768]{1,0:T(8,128)}, f32[192,3072]{1,0:T(8,128)}, f32[192,768]{1,0:T(8,128)}, f32[192,768]{1,0:T(8,128)}, f32[192,768]{1,0:T(8,128)}, /*inde...) custom-call(s32[2]{0:T(128)} %pad_add_fusion.3.place, ...), custom_call_target="tpu_custom_call" | custom-call | bytes 280000 | tf_op jit(solution)/shard_map/finish/pallas_call | solution.py:880
  (204 shorter events, 109.3 us)
Async XLA Ops:
  39.4 29.3 %all-to-all-start.1 = ((bf16[128,6,768]{2,1,0:T(8,128)(2,1)}), bf16[128,6,768]{2,1,0:T(8,128)(2,1)S(1)}, u32[]{:S(2)}, u32[]{:S(2)}) async-start(bf16[128,6,768]{2,1,0:T(8,128)(2,1)} %reshape.152), calls=%async_computation.1 | async-start | bytes 3145728 | tf_op jit(solution)/shard_map/all_to_all | solution.py:1013
  51.9 18.0 %collective-permute-start.2 = (bf16[144,768]{1,0:T(8,128)(2,1)S(1)}, bf16[144,768]{1,0:T(8,128)(2,1)S(1)}, u32[]{:S(2)}, u32[]{:S(2)}) collective-permute-start(bf16[144,768]{1,0:T(8,128)(2,1)S(1)} %get-tuple-element.225), channel_id=1, source_target_pairs={{1,0},{2,1},{3,2},{5,4},{6,5},{7,6},{9,8},{10,9},{11,10},{13,12},{... | collective-permute-start | bytes 663560 | tf_op jit(solution)/shard_map/ppermute | solution.py:951
  53.2 17.6 %collective-permute-start.1 = (bf16[144,768]{1,0:T(8,128)(2,1)S(1)}, bf16[144,768]{1,0:T(8,128)(2,1)S(1)}, u32[]{:S(2)}, u32[]{:S(2)}) collective-permute-start(bf16[144,768]{1,0:T(8,128)(2,1)S(1)} %get-tuple-element.226), channel_id=1, source_target_pairs={{0,2},{2,0},{3,1},{4,6},{6,4},{7,5},{8,10},{10,8},{11,9},{12,14},{... | collective-permute-start | bytes 663560 | tf_op jit(solution)/shard_map/ppermute | solution.py:951
  59.0 16.6 %collective-permute-start = (bf16[144,768]{1,0:T(8,128)(2,1)S(1)}, bf16[144,768]{1,0:T(8,128)(2,1)S(1)}, u32[]{:S(2)}, u32[]{:S(2)}) collective-permute-start(bf16[144,768]{1,0:T(8,128)(2,1)S(1)} %get-tuple-element.227), channel_id=1, source_target_pairs={{0,1},{1,2},{3,0},{4,5},{5,6},{7,4},{8,9},{9,10},{11,8},{12,13},{1... | collective-permute-start | bytes 663560 | tf_op jit(solution)/shard_map/ppermute | solution.py:951
  78.6 13.6 %collective-permute-start.3 = (bf16[128,768]{1,0:T(8,128)(2,1)}, bf16[128,768]{1,0:T(8,128)(2,1)S(1)}, u32[]{:S(2)}, u32[]{:S(2)}) collective-permute-start(bf16[128,768]{1,0:T(8,128)(2,1)} %get-tuple-element.128), channel_id=1, source_target_pairs={{0,1},{1,2},{3,0},{4,5},{5,6},{7,4},{8,9},{9,10},{11,8},{12,13},{1... | collective-permute-start | bytes 589832 | tf_op jit(solution)/shard_map/ppermute | solution.py:951
  80.6 11.6 %collective-permute-start.4 = (bf16[128,768]{1,0:T(8,128)(2,1)}, bf16[128,768]{1,0:T(8,128)(2,1)S(1)}, u32[]{:S(2)}, u32[]{:S(2)}) collective-permute-start(bf16[128,768]{1,0:T(8,128)(2,1)} %get-tuple-element.129), channel_id=1, source_target_pairs={{0,2},{2,0},{3,1},{4,6},{6,4},{7,5},{8,10},{10,8},{11,9},{12,14},{... | collective-permute-start | bytes 589832 | tf_op jit(solution)/shard_map/ppermute | solution.py:951
  82.5 9.6 %collective-permute-start.5 = (bf16[128,768]{1,0:T(8,128)(2,1)}, bf16[128,768]{1,0:T(8,128)(2,1)S(1)}, u32[]{:S(2)}, u32[]{:S(2)}) collective-permute-start(bf16[128,768]{1,0:T(8,128)(2,1)} %get-tuple-element.130), channel_id=1, source_target_pairs={{1,0},{2,1},{3,2},{5,4},{6,5},{7,6},{9,8},{10,9},{11,10},{13,12},{... | collective-permute-start | bytes 589832 | tf_op jit(solution)/shard_map/ppermute | solution.py:951
  134.6 9.5 %collective-permute-start.6 = (bf16[4,768,768]{2,1,0:T(8,128)(2,1)}, bf16[4,768,768]{2,1,0:T(8,128)(2,1)}, u32[]{:S(2)}, u32[]{:S(2)}) collective-permute-start(bf16[4,768,768]{2,1,0:T(8,128)(2,1)} %ff_send.1), channel_id=1, source_target_pairs={{0,4},{4,0},{8,12},{12,8},{16,20},{20,16},{24,28},{28,24},{32,36},... | collective-permute-start | bytes 14155784 | tf_op jit(solution)/shard_map/ppermute | solution.py:940
  153.2 28.9 %collective-permute-start.7 = (bf16[4,192,768]{2,1,0:T(8,128)(2,1)}, bf16[4,192,768]{2,1,0:T(8,128)(2,1)S(1)}, u32[]{:S(2)}, u32[]{:S(2)}) collective-permute-start(bf16[4,192,768]{2,1,0:T(8,128)(2,1)} %get-tuple-element.171), channel_id=1, source_target_pairs={{0,8},{4,36},{8,16},{12,44},{16,24},{20,52},{24,0},{28,60},{32,40}... | collective-permute-start | bytes 3538952 | tf_op jit(solution)/shard_map/ppermute | solution.py:928
  153.8 28.9 %collective-permute-start.8 = (bf16[4,192,768]{2,1,0:T(8,128)(2,1)}, bf16[4,192,768]{2,1,0:T(8,128)(2,1)S(1)}, u32[]{:S(2)}, u32[]{:S(2)}) collective-permute-start(bf16[4,192,768]{2,1,0:T(8,128)(2,1)} %get-tuple-element.172), channel_id=1, source_target_pairs={{0,16},{4,68},{8,24},{12,76},{16,0},{20,84},{24,8},{28,92},{32,48}... | collective-permute-start | bytes 3538952 | tf_op jit(solution)/shard_map/ppermute | solution.py:928
  156.0 27.2 %collective-permute-start.9 = (bf16[4,192,768]{2,1,0:T(8,128)(2,1)}, bf16[4,192,768]{2,1,0:T(8,128)(2,1)S(1)}, u32[]{:S(2)}, u32[]{:S(2)}) collective-permute-start(bf16[4,192,768]{2,1,0:T(8,128)(2,1)} %get-tuple-element.173), channel_id=1, source_target_pairs={{0,24},{4,100},{8,0},{12,108},{16,8},{20,116},{24,16},{28,124},{32... | collective-permute-start | bytes 3538952 | tf_op jit(solution)/shard_map/ppermute | solution.py:928
  183.2 11.9 %collective-permute-start.10 = (bf16[4,512,768]{2,1,0:T(8,128)(2,1)}, bf16[4,512,768]{2,1,0:T(8,128)(2,1)S(1)}, u32[]{:S(2)}, u32[]{:S(2)}) collective-permute-start(bf16[4,512,768]{2,1,0:T(8,128)(2,1)} %get-tuple-element.176), channel_id=1, source_target_pairs={{0,4},{4,0},{8,12},{12,8},{16,20},{20,16},{24,28},{28,24},{32,36},... | collective-permute-start | bytes 9437192 | tf_op jit(solution)/shard_map/ppermute | solution.py:940
  184.9 21.3 %collective-permute-start.14 = (bf16[144,768]{1,0:T(8,128)(2,1)}, bf16[144,768]{1,0:T(8,128)(2,1)S(1)}, u32[]{:S(2)}, u32[]{:S(2)}) collective-permute-start(bf16[144,768]{1,0:T(8,128)(2,1)} %get-tuple-element.189), channel_id=1, source_target_pairs={{1,0},{2,1},{0,3},{5,4},{6,5},{4,7},{9,8},{10,9},{8,11},{13,12},{1... | collective-permute-start | bytes 663560 | tf_op jit(solution)/shard_map/ppermute | solution.py:959
  188.0 18.2 %collective-permute-start.15 = (bf16[144,768]{1,0:T(8,128)(2,1)}, bf16[144,768]{1,0:T(8,128)(2,1)}, u32[]{:S(2)}, u32[]{:S(2)}) collective-permute-start(bf16[144,768]{1,0:T(8,128)(2,1)} %get-tuple-element.190), channel_id=1, source_target_pairs={{2,0},{0,2},{1,3},{6,4},{4,6},{5,7},{10,8},{8,10},{9,11},{14,12},{... | collective-permute-start | bytes 663560 | tf_op jit(solution)/shard_map/ppermute | solution.py:959
  192.9 13.3 %collective-permute-start.16 = (bf16[144,768]{1,0:T(8,128)(2,1)}, bf16[144,768]{1,0:T(8,128)(2,1)}, u32[]{:S(2)}, u32[]{:S(2)}) collective-permute-start(bf16[144,768]{1,0:T(8,128)(2,1)} %get-tuple-element.191), channel_id=1, source_target_pairs={{0,1},{1,2},{2,3},{4,5},{5,6},{6,7},{8,9},{9,10},{10,11},{12,13},{... | collective-permute-start | bytes 663560 | tf_op jit(solution)/shard_map/ppermute | solution.py:959
  213.8 58.3 %all-to-all-start.2 = ((bf16[128,6,768]{2,1,0:T(8,128)(2,1)}), bf16[128,6,768]{2,1,0:T(8,128)(2,1)S(1)}, u32[]{:S(2)}, u32[]{:S(2)}) async-start(bf16[128,6,768]{2,1,0:T(8,128)(2,1)} %reshape.165), calls=%async_computation.2 | async-start | bytes 3145728 | tf_op jit(solution)/shard_map/all_to_all | solution.py:1126
  218.9 34.8 %collective-permute-start.17 = (bf16[4,128,768]{2,1,0:T(8,128)(2,1)}, bf16[4,128,768]{2,1,0:T(8,128)(2,1)S(1)}, u32[]{:S(2)}, u32[]{:S(2)}) collective-permute-start(bf16[4,128,768]{2,1,0:T(8,128)(2,1)} %get-tuple-element.193), channel_id=1, source_target_pairs={{0,8},{4,36},{8,16},{12,44},{16,24},{20,52},{24,0},{28,60},{32,40}... | collective-permute-start | bytes 2359304 | tf_op jit(solution)/shard_map/ppermute | solution.py:928
  220.3 42.0 %collective-permute-start.18 = (bf16[4,128,768]{2,1,0:T(8,128)(2,1)}, bf16[4,128,768]{2,1,0:T(8,128)(2,1)S(1)}, u32[]{:S(2)}, u32[]{:S(2)}) collective-permute-start(bf16[4,128,768]{2,1,0:T(8,128)(2,1)} %get-tuple-element.194), channel_id=1, source_target_pairs={{0,16},{4,68},{8,24},{12,76},{16,0},{20,84},{24,8},{28,92},{32,48}... | collective-permute-start | bytes 2359304 | tf_op jit(solution)/shard_map/ppermute | solution.py:928
  222.8 39.6 %collective-permute-start.19 = (bf16[4,128,768]{2,1,0:T(8,128)(2,1)S(1)}, bf16[4,128,768]{2,1,0:T(8,128)(2,1)S(1)}, u32[]{:S(2)}, u32[]{:S(2)}) collective-permute-start(bf16[4,128,768]{2,1,0:T(8,128)(2,1)S(1)} %copy-done.45), channel_id=1, source_target_pairs={{0,24},{4,100},{8,0},{12,108},{16,8},{20,116},{24,16},{28,124},{32... | collective-permute-start | bytes 2359304 | tf_op jit(solution)/shard_map/ppermute | solution.py:928
  223.9 46.9 %collective-permute-start.11 = (bf16[4,48,768]{2,1,0:T(8,128)(2,1)}, bf16[4,48,768]{2,1,0:T(8,128)(2,1)S(1)}, u32[]{:S(2)}, u32[]{:S(2)}) collective-permute-start(bf16[4,48,768]{2,1,0:T(8,128)(2,1)} %get-tuple-element.183), channel_id=1, source_target_pairs={{0,32},{4,12},{8,40},{12,20},{16,48},{20,28},{24,56},{28,4},{32,64... | collective-permute-start | bytes 884744 | tf_op jit(solution)/shard_map/ppermute | solution.py:932
  225.1 48.2 %collective-permute-start.12 = (bf16[4,48,768]{2,1,0:T(8,128)(2,1)}, bf16[4,48,768]{2,1,0:T(8,128)(2,1)S(1)}, u32[]{:S(2)}, u32[]{:S(2)}) collective-permute-start(bf16[4,48,768]{2,1,0:T(8,128)(2,1)} %get-tuple-element.184), channel_id=1, source_target_pairs={{0,64},{4,20},{8,72},{12,28},{16,80},{20,4},{24,88},{28,12},{32,96... | collective-permute-start | bytes 884744 | tf_op jit(solution)/shard_map/ppermute | solution.py:932
  253.7 19.6 %collective-permute-start.13 = (bf16[4,48,768]{2,1,0:T(8,128)(2,1)}, bf16[4,48,768]{2,1,0:T(8,128)(2,1)S(1)}, u32[]{:S(2)}, u32[]{:S(2)}) collective-permute-start(bf16[4,48,768]{2,1,0:T(8,128)(2,1)} %get-tuple-element.185), channel_id=1, source_target_pairs={{0,96},{4,28},{8,104},{12,4},{16,112},{20,12},{24,120},{28,20},{32... | collective-permute-start | bytes 884744 | tf_op jit(solution)/shard_map/ppermute | solution.py:932
  292.8 12.7 %collective-permute-start.28 = (bf16[96,768]{1,0:T(8,128)(2,1)}, bf16[96,768]{1,0:T(8,128)(2,1)S(1)}, u32[]{:S(2)}, u32[]{:S(2)}) collective-permute-start(bf16[96,768]{1,0:T(8,128)(2,1)} %piece_rows.1.p0), channel_id=1, source_target_pairs={{0,96},{4,28},{8,104},{12,4},{16,112},{20,12},{24,120},{28,20},{32... | collective-permute-start | bytes 442376 | tf_op jit(solution)/shard_map/ppermute | solution.py:932
  293.5 12.0 %collective-permute-start.27 = (bf16[96,768]{1,0:T(8,128)(2,1)}, bf16[96,768]{1,0:T(8,128)(2,1)S(1)}, u32[]{:S(2)}, u32[]{:S(2)}) collective-permute-start(bf16[96,768]{1,0:T(8,128)(2,1)} %piece_rows.1.p0), channel_id=1, source_target_pairs={{0,64},{4,20},{8,72},{12,28},{16,80},{20,4},{24,88},{28,12},{32,96... | collective-permute-start | bytes 442376 | tf_op jit(solution)/shard_map/ppermute | solution.py:932
  296.0 9.6 %collective-permute-start.26 = (bf16[96,768]{1,0:T(8,128)(2,1)}, bf16[96,768]{1,0:T(8,128)(2,1)S(1)}, u32[]{:S(2)}, u32[]{:S(2)}) collective-permute-start(bf16[96,768]{1,0:T(8,128)(2,1)} %piece_rows.1.p0), channel_id=1, source_target_pairs={{0,32},{4,12},{8,40},{12,20},{16,48},{20,28},{24,56},{28,4},{32,64... | collective-permute-start | bytes 442376 | tf_op jit(solution)/shard_map/ppermute | solution.py:932
  308.9 9.2 %collective-permute-start.31 = (bf16[384,768]{1,0:T(8,128)(2,1)}, bf16[384,768]{1,0:T(8,128)(2,1)S(1)}, u32[]{:S(2)}, u32[]{:S(2)}) collective-permute-start(bf16[384,768]{1,0:T(8,128)(2,1)} %bitcast.39), channel_id=1, source_target_pairs={{0,24},{4,100},{8,0},{12,108},{16,8},{20,116},{24,16},{28,124},{32... | collective-permute-start | bytes 1769480 | tf_op jit(solution)/shard_map/ppermute | solution.py:928
  308.9 10.8 %collective-permute-start.30 = (bf16[384,768]{1,0:T(8,128)(2,1)}, bf16[384,768]{1,0:T(8,128)(2,1)S(1)}, u32[]{:S(2)}, u32[]{:S(2)}) collective-permute-start(bf16[384,768]{1,0:T(8,128)(2,1)} %bitcast.40), channel_id=1, source_target_pairs={{0,16},{4,68},{8,24},{12,76},{16,0},{20,84},{24,8},{28,92},{32,48}... | collective-permute-start | bytes 1769480 | tf_op jit(solution)/shard_map/ppermute | solution.py:928
  309.0 17.0 %collective-permute-start.29 = (bf16[384,768]{1,0:T(8,128)(2,1)}, bf16[384,768]{1,0:T(8,128)(2,1)S(1)}, u32[]{:S(2)}, u32[]{:S(2)}) collective-permute-start(bf16[384,768]{1,0:T(8,128)(2,1)} %bitcast.41), channel_id=1, source_target_pairs={{0,8},{4,36},{8,16},{12,44},{16,24},{20,52},{24,0},{28,60},{32,40}... | collective-permute-start | bytes 1769480 | tf_op jit(solution)/shard_map/ppermute | solution.py:928
  329.9 20.9 %collective-permute-start.35 = (bf16[4,384,768]{2,1,0:T(8,128)(2,1)}, bf16[4,384,768]{2,1,0:T(8,128)(2,1)S(1)}, u32[]{:S(2)}, u32[]{:S(2)}) collective-permute-start(bf16[4,384,768]{2,1,0:T(8,128)(2,1)} %order.3.own), channel_id=1, source_target_pairs={{0,4},{4,0},{8,12},{12,8},{16,20},{20,16},{24,28},{28,24},{32,36},... | collective-permute-start | bytes 7077896 | tf_op jit(solution)/shard_map/ppermute | solution.py:940
  333.1 12.4 %collective-permute-start.32 = (bf16[128,768]{1,0:T(8,128)(2,1)S(1)}, bf16[128,768]{1,0:T(8,128)(2,1)S(1)}, u32[]{:S(2)}, u32[]{:S(2)}) collective-permute-start(bf16[128,768]{1,0:T(8,128)(2,1)S(1)} %copy-done.48), channel_id=1, source_target_pairs={{1,0},{2,1},{0,3},{5,4},{6,5},{4,7},{9,8},{10,9},{8,11},{13,12},{1... | collective-permute-start | bytes 589832 | tf_op jit(solution)/shard_map/ppermute | solution.py:959
  337.1 9.6 %collective-permute-start.33 = (bf16[128,768]{1,0:T(8,128)(2,1)S(1)}, bf16[128,768]{1,0:T(8,128)(2,1)S(1)}, u32[]{:S(2)}, u32[]{:S(2)}) collective-permute-start(bf16[128,768]{1,0:T(8,128)(2,1)S(1)} %copy-done.47), channel_id=1, source_target_pairs={{2,0},{0,2},{1,3},{6,4},{4,6},{5,7},{10,8},{8,10},{9,11},{14,12},{... | collective-permute-start | bytes 589832 | tf_op jit(solution)/shard_map/ppermute | solution.py:959
  339.8 8.2 %collective-permute-start.34 = (bf16[128,768]{1,0:T(8,128)(2,1)S(1)}, bf16[128,768]{1,0:T(8,128)(2,1)S(1)}, u32[]{:S(2)}, u32[]{:S(2)}) collective-permute-start(bf16[128,768]{1,0:T(8,128)(2,1)S(1)} %copy-done.46), channel_id=1, source_target_pairs={{0,1},{1,2},{2,3},{4,5},{5,6},{6,7},{8,9},{9,10},{10,11},{12,13},{... | collective-permute-start | bytes 589832 | tf_op jit(solution)/shard_map/ppermute | solution.py:959
  (56 other events, 387.7 us)
where the time goes:
time: 371 us; the launch traced here: 363 us
  Pallas kernels  136 us (37%)
  waiting for transfers between devices  87.7 us (24%)
  starting transfers between devices  77.8 us (21%)
  local copies, waits for them, and re-layouts  34.4 us (9%)
  blocking collectives  21.1 us (6%)
  other arithmetic  4.69 us (1%)
    ppermute x9, waiting for transfers between devices, shift_first(): return lax.ppermute(array, 'batch', shift_pairs(step, 'xy'))  46.2 us
    pallas_call x1, Pallas kernels, attn_bwd(): pl.pallas_call(attn_bwd_kernel, grid_spec=prefetch(1, (steps,), ins + [pl...  24.6 us
    pallas_call x1, Pallas kernels, feed_forward(): pl.pallas_call(functools.partial(ff_kernel, chunk=chunk), grid_spec=prefe...  23 us
    all_to_all x1, blocking collectives, per_device(): lax.all_to_all(requests, ('batch', 'seq'), split_axis=0, concat_axis=0, t...  21.1 us
    ppermute x6, starting transfers between devices, from_sentence(): out.append(lax.ppermute(parts[step], 'seq', pairs))  18.1 us
    ppermute x6, starting transfers between devices, to_sentence(): out.append(lax.ppermute(parts[step], 'seq', pairs))  14.5 us
    ppermute x9, starting transfers between devices, shift_second(): return lax.ppermute(array, 'batch', shift_pairs(step, 'yx'))  13.9 us
    ppermute x6, waiting for transfers between devices, to_sentence(): out.append(lax.ppermute(parts[step], 'seq', pairs))  12.4 us
  transfers between devices with their start and end apart: 38, of which 20 were waited for; matrix products, arithmetic and copies ran while one was open for 4% of the time, Pallas kernels for 14%

commit v1 on v0

--- a/solution.py
+++ b/solution.py
@@ -11,7 +11,7 @@
 EPSILON = 1e-12
 MASKED = -1000000000.0
 HEAD_DIM = 64
-VMEM = 56 * 1024 * 1024
+VMEM = 63 * 1024 * 1024
 HALF = 384
 SHARE = 0.02
 
@@ -84,8 +84,8 @@
 
 
 def attn_fwd(parts, wq, wk, wv, bq, bv, live, group=256):
-    n, d = parts[0].shape
-    s = 4 * n
+    s, d = live.shape[0], wq.shape[0]
+    n = s // 4
     hg = group // HEAD_DIM
     col = pl.BlockSpec((s, group), lambda h: (0, h))
     wcol = pl.BlockSpec((d, group), lambda h: (0, h))
@@ -94,7 +94,7 @@
     return pl.pallas_call(
         attn_fwd_kernel,
         grid=(d // group,),
-        in_specs=[whole((n, d))] * 4 + [wcol, wcol, wcol, brow, brow, whole((s, 1))],
+        in_specs=[pl.BlockSpec((n, d), lambda h: (0, 0))] * 4 + [wcol, wcol, wcol, brow, brow, whole((s, 1))],
         out_specs=[
             whole((s, d)),
             col,
@@ -164,7 +164,7 @@
 
 def attn_bwd_kernel(
     place, al, wo, q, k, v, e_i, inv_i, mt_i, wq_a, wk_a, wv_a, x_a, base_a, mixed_a,
-    pool, vec1, vec2, ib, p0, p1, p2, p3, send, keep,
+    res0, res1, res2, res3, pool, vec1, vec2, ib, p0, p1, p2, p3, send, keep,
     dm, dq, dk, dv, wq, wk, wv, x, base, mixed, eg, sems
 ):
     pairs = ((wq_a, wq), (wk_a, wk), (wv_a, wv), (x_a, x), (base_a, base), (mixed_a, mixed))
@@ -204,8 +204,9 @@
             at = slice(m * n, m * n + n)
             value = (base[at, :] + embed_part(dq, dk, dv, wq, wk, wv, at)).astype(LOW)
             eg[m] = value
-            part[n : n + 16, :] = pool[...]
             part[0:n, :] = value
+            part[n : 2 * n, :] = (res0, res1, res2, res3)[m][...]
+            part[2 * n : 2 * n + 16, :] = pool[...]
         put(0, slice(2 * share, 2 * share + n), lambda z: eg[(place[0] + 4 - z) % 4])
         vectors = [
             jnp.sum(dq[...].astype(F32), axis=0, keepdims=True) * scale,
@@ -222,12 +223,13 @@
         put(1, slice(2 * share, 2 * share + n), lambda z: vectors)
 
 
-def attn_bwd(place, al, wo, q, k, v, e, inv, mt, wq, wk, wv, x, base, mixed, pool, vec1, vec2, ib):
+def attn_bwd(place, al, wo, q, k, v, e, inv, mt, wq, wk, wv, x, base, mixed, res, pool, vec1, vec2, ib):
     s, d = q.shape
     steps = d // 128
     heads = d // HEAD_DIM
     col = pl.BlockSpec((s, 128), lambda h, p: (0, h))
-    small = [whole(pool.shape), whole(vec1.shape), whole(vec2.shape), whole(ib.shape)]
+    small = [whole(part.shape) for part in res]
+    small += [whole(pool.shape), whole(vec1.shape), whole(vec2.shape), whole(ib.shape)]
     ins = [
         whole((s, d)),
         whole((d, d)),
@@ -238,7 +240,7 @@
         pl.BlockSpec((2, 1, s), lambda h, p: (h, 0, 0)),
         pl.BlockSpec((128, s), lambda h, p: (h, 0)),
     ]
-    shapes = [((s // 4 + 16, d), LOW)] * 4 + [((4, d // 2 + s // 4, d), LOW)] * 2
+    shapes = [((s // 2 + 16, d), LOW)] * 4 + [((4, d // 2 + s // 4, d), LOW)] * 2
     return pl.pallas_call(
         attn_bwd_kernel,
         grid_spec=prefetch(
@@ -255,7 +257,7 @@
         compiler_params=params(),
         cost_estimate=cost(14 * s * d * d + 8 * s * s * 256 * heads, 28e6),
         name="attention_backward",
-    )(place, al, wo, q, k, v, e, inv, mt, wq, wk, wv, x, base, mixed, pool, vec1, vec2, ib)
+    )(place, al, wo, q, k, v, e, inv, mt, wq, wk, wv, x, base, mixed, *res, pool, vec1, vec2, ib)
 
 
 def normalize(values):
@@ -299,7 +301,8 @@
 
     loads = [pltpu.make_async_copy(wp, wps, sems.at[2 * blocks])]
     for m, part in enumerate((u0, u1, u2, u3)):
-        loads.append(pltpu.make_async_copy(part, ups.at[m], sems.at[2 * blocks + 1 + m]))
+        rows = part.at[pl.ds(n, n + 16), :]
+        loads.append(pltpu.make_async_copy(rows, ups.at[m], sems.at[2 * blocks + 1 + m]))
     for f in range(blocks):
         load1(f).start()
         load2(f).start()
@@ -559,32 +562,37 @@
     )(fetch, table)
 
 
-def embed_kernel(place, slot, replies, pos, o0, o1, o2, o3):
+def embed_kernel(place, slot, replies, pos, grads, terms, o0, o1, o2, o3):
+    n = pos.shape[0]
     ids = lax.broadcasted_iota(jnp.int32, (1, replies.shape[0]), 1)
     for m, out in enumerate((o0, o1, o2, o3)):
         sent = (place[0] + m) % 4
+        here = jnp.minimum(sent, 2)
         hot = jnp.where(ids == slot[sent], 1.0, 0.0).astype(LOW)
         live = jnp.where(sent < 3, 1.0, 0.0)
-        out[...] = ((nn(hot, replies[...]) + pos[...].astype(F32)) * live).astype(LOW)
-
-
-def embed_parts(place, slot, replies, pos):
+        out[0:n, :] = ((nn(hot, replies[...]) + pos[...].astype(F32)) * live).astype(LOW)
+        out[n : 2 * n, :] = (grads[here].astype(F32) * live).astype(LOW)
+        out[2 * n : 2 * n + 16, :] = (terms[here].astype(F32) * live).astype(LOW)
+
+
+def embed_parts(place, slot, replies, pos, grads, terms):
     slots, d = replies.shape
     n = pos.shape[0]
-    out = pl.BlockSpec((n, d), lambda i, p: (0, 0))
+    out = (2 * n + 16, d)
     return pl.pallas_call(
         embed_kernel,
         grid_spec=prefetch(
             1,
             (1,),
-            [whole((4, n, 1)), whole((slots, d)), whole((n, d))],
-            [out] * 4,
+            [whole((4, n, 1)), whole((slots, d)), whole((n, d))]
+            + [whole(grads.shape), whole(terms.shape)],
+            [whole(out)] * 4,
         ),
-        out_shape=[struct((n, d), LOW)] * 4,
+        out_shape=[struct(out, LOW)] * 4,
         compiler_params=params(),
         cost_estimate=cost(2 * slots * 4 * n * d, 3e6),
         name="embed_parts",
-    )(place, slot, replies, pos)
+    )(place, slot, replies, pos, grads, terms)
 
 
 def outgoing_kernel(place, slot, p0, p1, p2, p3, out):
@@ -603,7 +611,10 @@
     return pl.pallas_call(
         outgoing_kernel,
         grid_spec=prefetch(
-            1, (1,), [whole((4, 1, n))] + [whole((n, d))] * 4, whole((slots, d))
+            1,
+            (1,),
+            [whole((4, 1, n))] + [pl.BlockSpec((n, d), lambda i, p: (0, 0))] * 4,
+            whole((slots, d)),
         ),
         out_shape=struct((slots, d), LOW),
         compiler_params=params(),
@@ -645,7 +656,9 @@
     d = parts[0].shape[1]
     return pl.pallas_call(
         unpermute_kernel,
-        grid_spec=prefetch(1, (1,), [whole((n, d))] * 4, whole((3, n, d))),
+        grid_spec=prefetch(
+            1, (1,), [pl.BlockSpec((n, d), lambda i, p: (1, 0))] * 4, whole((3, n, d))
+        ),
         out_shape=struct((3, n, d), parts[0].dtype),
         compiler_params=params(),
         cost_estimate=cost(0, 2e6),
@@ -800,7 +813,7 @@
         piece_kernel,
         grid=(1,),
         in_specs=[whole(p.shape) for p in parts]
-        + [pl.BlockSpec((16, d), lambda i: (8, 0)) for p in pool],
+        + [pl.BlockSpec((16, d), lambda i: (16, 0)) for p in pool],
         out_specs=whole((96, d)),
         out_shape=struct((96, d), LOW),
         compiler_params=params(),
@@ -904,7 +917,7 @@
 
 def pooled_rows(place, parts):
     d = parts[0].shape[1]
-    below = pl.BlockSpec((16, d), lambda i, p: (8, 0))
+    below = pl.BlockSpec((16, d), lambda i, p: (16, 0))
     return pl.pallas_call(
         pooled_kernel,
         grid_spec=prefetch(1, (1,), [below] * 4, whole((4, 8, d))),
@@ -1042,17 +1055,13 @@
     high = pooled_grad.astype(LOW)
     terms = jnp.stack([high, (pooled_grad - high.astype(F32)).astype(LOW)], axis=1)
     terms = jnp.pad(terms, ((0, 0), (0, 14), (0, width - terms.shape[2])))
-    cotangents = jnp.concatenate([out_grad, terms], axis=1)
-    early = [live_keys] + [row(v) for v in vectors]
-    cotangents, *early = lax.optimization_barrier([cotangents] + early)
-    live_keys, q_bias, v_bias, o_bias, gain1, shift1, in_bias, out_bias, gain2, shift2, pool_bias = early
-    ups = [
-        lax.dynamic_index_in_dim(cotangents, jnp.minimum((z + m) % 4, 2), 0, keepdims=False)
-        for m in range(4)
-    ]
-    ups = to_sentence([jnp.where(z < 3, ups[0], jnp.zeros((), LOW))] + ups[1:])
-    replies, *ups = lax.optimization_barrier([replies] + ups)
-    embeds = to_sentence(embed_parts(scalars(z), slot_cols, replies, positions))
+    early = [live_keys, terms] + [row(v) for v in vectors]
+    replies, *early = lax.optimization_barrier([replies] + early)
+    live_keys, terms = early[:2]
+    q_bias, v_bias, o_bias, gain1, shift1, in_bias, out_bias, gain2, shift2, pool_bias = early[2:]
+    embeds = to_sentence(
+        embed_parts(scalars(z), slot_cols, replies, positions, out_grad, terms)
+    )
 
     embed, query, key, value, expo, inverse, mixed_t, mixed = attn_fwd(
         embeds, query_weight, key_weight, value_weight, q_bias, v_bias, live_keys
@@ -1083,7 +1092,7 @@
         shift2,
         pooler_weight,
         pool_bias,
-        ups,
+        embeds,
     )
 
     ff_other = ff_send(scalars(1 - core), left, right)
@@ -1106,6 +1115,7 @@
         embed,
         first_back,
         mixed,
+        result,
         pool,
         vec1,
         vec2,
@@ -1120,36 +1130,37 @@
     ff_parts[0] = tie(ff_parts[0], rest_parts[0])
     rest_parts = ring_send(rest_parts, shift_first)
     ff_parts = ring_add(scalars(second), ff_parts)
-    returned[0] = tie(returned[0], ff_parts[0])
+    rest_parts[0] = tie(rest_parts[0], ff_parts[0])
+    ff_parts = ring_send(ff_parts, shift_second)
+    rest_parts = ring_add(scalars(second), rest_parts)
+    returned[0] = tie(returned[0], rest_parts[0])
     outgoing = outgoing_rows(scalars(z), slot_rows, returned, all_slots)
-    ff_parts = ring_send(ff_parts, shift_second)
+    outgoing = outgoing.reshape(all_count, slots, width)
+    rest_parts = ring_send(rest_parts, shift_second)
+    rest_parts[0] = tie(rest_parts[0], outgoing)
+    parts = ring_send(join(scalars(z), ff_parts, rest_parts), shift_z)
+    piece = piece_rows(parts, returned)
+    pieces = [piece] + [shift_second(piece, m) for m in (1, 2, 3)]
+    pooled = pooled_rows(scalars(z), [tie(returned[0], piece)] + returned[1:])
+    pooled = pooled[:num_sent, 0, : width // 4]
+    hidden_out = unpermute(scalars(z), [tie(returned[0], piece)] + returned[1:], local_len)
+    pieces[0] = tie(pieces[0], pooled, hidden_out)
+    block = order(scalars(second), pieces).reshape(-1, width)
+    blocks = [block] + [shift_first(block, m) for m in (1, 2, 3)]
     incoming = lax.all_to_all(
-        outgoing.reshape(all_count, slots, width),
+        tie(outgoing, block),
         ("batch", "seq"),
         split_axis=0,
         concat_axis=0,
         tiled=True,
     ).reshape(all_slots, width)
-    rest_parts[0] = tie(rest_parts[0], outgoing)
-    rest_parts = ring_send(ring_add(scalars(second), rest_parts), shift_second)
-    rest_parts[0] = tie(rest_parts[0], incoming)
-    parts = ring_send(join(scalars(z), ff_parts, rest_parts), shift_z)
-    piece = piece_rows(parts, returned)
-    incoming = tie(incoming, piece)
-    pieces = [piece] + [shift_second(piece, m) for m in (1, 2, 3)]
     grad_table = table_grad(fetch[None, :], incoming, table_rows)
-    pieces[0] = tie(pieces[0], grad_table)
-    block = order(scalars(second), pieces).reshape(-1, width)
-    result[0] = tie(result[0], block)
-    blocks = [block] + [shift_first(block, m) for m in (1, 2, 3)]
-    result = from_sentence(result)
-    pooled = pooled_rows(scalars(z), [tie(returned[0], block)] + returned[1:])
-    pooled = pooled[:num_sent, 0, : width // 4]
-    blocks[0] = tie(blocks[0], pooled)
+    blocks[0] = tie(blocks[0], incoming)
     whole_own = order(scalars(first), blocks)
+    incoming = tie(incoming, whole_own)
     whole_other = swap_core(whole_own)
-    result[0] = tie(result[0], whole_own)
-    hidden_out = unpermute(scalars(z), result, local_len)
+    grad_table = table_grad(fetch[None, :], incoming, table_rows)
+    whole_other = tie(whole_other, grad_table)
     (
         grad_outer,
         grad_inner,
@@ -1161,7 +1172,7 @@
         vectors,
         grad_pooler,
         pooler_bias_grad,
-    ) = finish(scalars(core, z), tie(whole_own, hidden_out), whole_other)
+    ) = finish(scalars(core, z), whole_own, whole_other)
 
     share = width // 4
     mine = lax.dynamic_slice_in_dim(vectors[:8], z * share, share, 1)

time: 371 us -> 343 us (0.925)
  starting transfers between devices: 77.8 us -> 61.2 us
  local copies, waits for them, and re-layouts: 34.4 us -> 26.4 us
    ppermute x9, waiting for transfers between devices: 46.2 us -> 8.55 us  [shift_first(): return lax.ppermute(array, 'batch', shift_pairs(step, 'xy'))]
    all_to_all x1, waiting for transfers between devices: 0.01 us -> 21 us  [per_device(): lax.all_to_all(tie(outgoing, block), ('batch', 'seq'), split_axis=0, conc...]
    all_to_all x1, waiting for transfers between devices: 7.75 us -> 17 us  [per_device(): lax.all_to_all(found.reshape(all_count, slots, width), ('batch', 'seq'),...]
    unnamed x101 -> x51, local copies, waits for them, and re-layouts: 11.8 us -> 3.15 us
    ppermute x6 -> x3, starting transfers between devices: 14.5 us -> 5.83 us  [to_sentence(): out.append(lax.ppermute(parts[step], 'seq', pairs))]
    all_to_all x1, starting transfers between devices: 5.11 us -> 12.1 us  [per_device(): lax.all_to_all(tie(outgoing, block), ('batch', 'seq'), split_axis=0, conc...]
    ppermute x6 -> x3, starting transfers between devices: 18.1 us -> 11.4 us  [from_sentence(): out.append(lax.ppermute(parts[step], 'seq', pairs))]
    ppermute x3, waiting for transfers between devices: 7.3 us -> 12.9 us  [swap_core(): return lax.ppermute(array, 'batch', [(i, i ^ 1) for i in range(32)])]
  transfers between devices with their start and end apart: 38 -> 32, of which waited for: 20 -> 13; matrix products, arithmetic and copies ran while one was open for 4% -> 5% of each run, Pallas kernels for 14% -> 14%
where the time goes in v1:
time: 343 us; the launch traced here: 337 us
  Pallas kernels  137 us (40%)
  waiting for transfers between devices  85.7 us (25%)
  starting transfers between devices  61.2 us (18%)
  local copies, waits for them, and re-layouts  26.4 us (8%)
  blocking collectives  21.1 us (6%)
  other arithmetic  3.95 us (1%)
    pallas_call x1, Pallas kernels, attn_bwd(): pl.pallas_call(attn_bwd_kernel, grid_spec=prefetch(1, (steps,), ins + [pl...  25.1 us
    pallas_call x1, Pallas kernels, feed_forward(): pl.pallas_call(functools.partial(ff_kernel, chunk=chunk), grid_spec=prefe...  23 us
    all_to_all x1, blocking collectives, per_device(): lax.all_to_all(requests, ('batch', 'seq'), split_axis=0, concat_axis=0, t...  21.1 us
    all_to_all x1, waiting for transfers between devices, per_device(): lax.all_to_all(tie(outgoing, block), ('batch', 'seq'), split_axis=0, conc...  21 us
    all_to_all x1, waiting for transfers between devices, per_device(): lax.all_to_all(found.reshape(all_count, slots, width), ('batch', 'seq'),...  17 us
    ppermute x3, waiting for transfers between devices, to_sentence(): out.append(lax.ppermute(parts[step], 'seq', pairs))  15.8 us
    ppermute x3, waiting for transfers between devices, swap_core(): return lax.ppermute(array, 'batch', [(i, i ^ 1) for i in range(32)])  12.9 us
    all_to_all x1, starting transfers between devices, per_device(): lax.all_to_all(tie(outgoing, block), ('batch', 'seq'), split_axis=0, conc...  12.1 us
  transfers between devices with their start and end apart: 32, of which 13 were waited for; matrix products, arithmetic and copies ran while one was open for 5% of the time, Pallas kernels for 14%

profile of v1, /device:TPU:1, one launch (start us, length us, event | category | flops | bytes accessed | tf_op | source)
XLA Modules:
  0.0 336.7 jit_solution(5633151162956433739)
XLA Ops:
  3.0 21.1 %all_to_all.19 = s32[128,1,6]{2,1,0:T(1,128)S(1)} all-to-all(s32[128,1,6]{2,1,0:T(1,128)} %bitcast.36), channel_id=1, replica_groups=mesh['batch'=32,'seq'=4] {'batch','seq'}, dimensions={0} | all-to-all | bytes 6144 | tf_op jit(solution)/shard_map/all_to_all | solution.py:1023
  26.3 9.8 %gather_rows.1 = bf16[768,768]{1,0:T(8,128)(2,1)} custom-call(s32[768,1]{1,0:T(8,128)} %broadcast_in_dim_reshape.8.fetch, bf16[3912,768]{1,0:T(8,128)(2,1)} %table.1), custom_call_target="tpu_custom_call" | custom-call | flops 92295656 | bytes 160000 | tf_op jit(solution)/shard_map/gather_rows/pallas_call | solution.py:552
  36.0 3.2 reshape.149
  39.3 4.3 %all-to-all-start.1 = ((bf16[128,6,768]{2,1,0:T(8,128)(2,1)}), bf16[128,6,768]{2,1,0:T(8,128)(2,1)S(1)}, u32[]{:S(2)}, u32[]{:S(2)}) async-start(bf16[128,6,768]{2,1,0:T(8,128)(2,1)} %reshape.149), calls=%async_computation.1 | async-start | bytes 3145728 | tf_op jit(solution)/shard_map/all_to_all | solution.py:1026
  51.6 17.0 %all-to-all-done.1 = bf16[128,6,768]{2,1,0:T(8,128)(2,1)S(1)} async-done(((bf16[128,6,768]{2,1,0:T(8,128)(2,1)}), bf16[128,6,768]{2,1,0:T(8,128)(2,1)S(1)}, u32[]{:S(2)}, u32[]{:S(2)}) %all-to-all-start.1) | async-done | bytes 1179680 | tf_op jit(solution)/shard_map/all_to_all | solution.py:1026
  69.8 3.5 %embed_parts.1 = (bf16[272,768]{1,0:T(8,128)(2,1)}, bf16[272,768]{1,0:T(8,128)(2,1)}, bf16[272,768]{1,0:T(8,128)(2,1)}, bf16[272,768]{1,0:T(8,128)(2,1)}) custom-call(s32[1]{0:T(128)} %bitcast.place, s32[4,128,1]{2,1,0:T(8,128)} %get-tuple-element.118.slot, bf16[768,768]{1,0:T(8,128)(2,1)} %reshape.150.replies, bf16[128,768]{1,0:T(8,128)(2,1)} %pos.1, ...), custom_call_target="tpu_custom_call" | custom-call | flops 12079595 | bytes 60000 | tf_op jit(solution)/shard_map/embed_parts/pallas_call | solution.py:582
  80.6 15.7 %collective-permute-done.x1.u1 = bf16[272,768]{1,0:T(8,128)(2,1)S(1)} collective-permute-done((bf16[272,768]{1,0:T(8,128)(2,1)}, bf16[272,768]{1,0:T(8,128)(2,1)S(1)}, u32[]{:S(2)}, u32[]{:S(2)}) %collective-permute-start) | collective-permute-done | bytes 417824 | tf_op jit(solution)/shard_map/ppermute | solution.py:964
  97.3 12.0 %attention_forward.1 = (bf16[512,768]{1,0:T(8,128)(2,1)}, bf16[512,768]{1,0:T(8,128)(2,1)}, bf16[512,768]{1,0:T(8,128)(2,1)}, bf16[512,768]{1,0:T(8,128)(2,1)}, ...) custom-call(bf16[272,768]{1,0:T(8,128)(2,1)} %get-tuple-element.122., ...), custom_call_target="tpu_custom_call" | custom-call | flops 100663296 | bytes 320000 | tf_op jit(solution)/shard_map/attention_forward/pallas_call | solution.py:94
  109.3 23.0 %feed_forward.1 = (bf16[2,512,768]{2,1,0:T(8,128)(2,1)}, bf16[2,4,512,768]{3,2,1,0:T(8,128)(2,1)}, bf16[128,768]{1,0:T(8,128)(2,1)}, bf16[128,768]{1,0:T(8,128)(...) custom-call(s32[3]{0:T(128)} %pad_add_fusion.1.row0, ...), custom_call_target="tpu_custom_call" | custom-call | flops 205353120 | bytes 600000 | tf_op jit(solution)/shard_map/feed_forward/pallas_call | solution.py:413
  132.3 6.5 %ff_send.1 = bf16[4,768,768]{2,1,0:T(8,128)(2,1)} custom-call(s32[1]{0:T(128)} %bitcast.12.which, bf16[2,512,768]{2,1,0:T(8,128)(2,1)} %get-tuple-element.140.left, bf16[2,4,512,768]{3,2,1,0:T(8,128)(2,1)} %get-tuple-element.141.right), custom_call_target="tpu_custom_call" | custom-call | flops 48318384 | bytes 180000 | tf_op jit(solution)/shard_map/ff_send/pallas_call | solution.py:682
  140.9 7.3 %collective-permute-done.3.got = bf16[4,768,768]{2,1,0:T(8,128)(2,1)} collective-permute-done((bf16[4,768,768]{2,1,0:T(8,128)(2,1)}, bf16[4,768,768]{2,1,0:T(8,128)(2,1)}, u32[]{:S(2)}, u32[]{:S(2)}) %collective-permute-start.3) | collective-permute-done | bytes 4718624 | tf_op jit(solution)/shard_map/ppermute | solution.py:953
  148.2 9.2 %ff_keep.1 = (bf16[4,192,768]{2,1,0:T(8,128)(2,1)}, bf16[4,192,768]{2,1,0:T(8,128)(2,1)}, bf16[4,192,768]{2,1,0:T(8,128)(2,1)}, bf16[4,192,768]{2,1,0:T(8,128)(2,1)}) custom-call(s32[2]{0:T(128)} %get-tuple-element.226.place, bf16[2,512,768]{2,1,0:T(8,128)(2,1)} %get-tuple-element.140.left, bf16[2,4,512,768]{3,2,1,0:T(8,128)(2,1)} %get-tuple-element.141.right, ...), custom_call_target="tpu_custom_call" | custom-call | flops 48318384 | bytes 280000 | tf_op jit(solution)/shard_map/ff_keep/pallas_call | solution.py:717
  160.2 25.1 %attention_backward.1 = (bf16[272,768]{1,0:T(8,128)(2,1)}, bf16[272,768]{1,0:T(8,128)(2,1)}, bf16[272,768]{1,0:T(8,128)(2,1)}, bf16[272,768]{1,0:T(8,128)(2,1)},...) custom-call(s32[2]{0:T(128)} %get-tuple-element.225.place, bf16[512,768]{1,0:T(8,128)(2,1)} %get-tuple-element.143.al, ...), custom_call_target="tpu_custom_call" | custom-call | flops 213406192 | bytes 560000 | tf_op jit(solution)/shard_map/attention_backward/pallas_call | solution.py:244
  189.5 5.6 %collective-permute-done.7.got = bf16[4,512,768]{2,1,0:T(8,128)(2,1)} collective-permute-done((bf16[4,512,768]{2,1,0:T(8,128)(2,1)}, bf16[4,512,768]{2,1,0:T(8,128)(2,1)}, u32[]{:S(2)}, u32[]{:S(2)}) %collective-permute-start.7) | collective-permute-done | bytes 3145760 | tf_op jit(solution)/shard_map/ppermute | solution.py:953
  195.1 5.1 %core_add.1 = (bf16[4,128,768]{2,1,0:T(8,128)(2,1)}, bf16[4,128,768]{2,1,0:T(8,128)(2,1)}, bf16[4,128,768]{2,1,0:T(8,128)(2,1)}, bf16[4,128,768]{2,1,0:T(8,128)(2,1)}) custom-call(s32[1]{0:T(128)} %bitcast.11.place, bf16[4,512,768]{2,1,0:T(8,128)(2,1)} %get-tuple-element.169.own, bf16[4,512,768]{2,1,0:T(8,128)(2,1)} %collective-permute-done.7.got), custom_call_target="tpu_custom_call" | custom-call | bytes 180000 | tf_op jit(solution)/shard_map/core_add/pallas_call | solution.py:742
  203.0 2.6 collective-permute-start.14
  205.6 5.0 %collective-permute-start.15 = (bf16[272,768]{1,0:T(8,128)(2,1)}, bf16[272,768]{1,0:T(8,128)(2,1)S(1)}, u32[]{:S(2)}, u32[]{:S(2)}) collective-permute-start(bf16[272,768]{1,0:T(8,128)(2,1)} %get-tuple-element.189), channel_id=1, source_target_pairs={{2,0},{0,2},{1,3},{6,4},{4,6},{5,7},{10,8},{8,10},{9,11},{14,12},{... | collective-permute-start | bytes 1253384 | tf_op jit(solution)/shard_map/ppermute | solution.py:972
  210.6 4.9 %collective-permute-done.14.p1.r1 = bf16[272,768]{1,0:T(8,128)(2,1)S(1)} collective-permute-done((bf16[272,768]{1,0:T(8,128)(2,1)}, bf16[272,768]{1,0:T(8,128)(2,1)S(1)}, u32[]{:S(2)}, u32[]{:S(2)}) %collective-permute-start.14) | collective-permute-done | bytes 417824 | tf_op jit(solution)/shard_map/ppermute | solution.py:972
  215.6 3.8 %collective-permute-start.16 = (bf16[272,768]{1,0:T(8,128)(2,1)}, bf16[272,768]{1,0:T(8,128)(2,1)}, u32[]{:S(2)}, u32[]{:S(2)}) collective-permute-start(bf16[272,768]{1,0:T(8,128)(2,1)} %get-tuple-element.190), channel_id=1, source_target_pairs={{0,1},{1,2},{2,3},{4,5},{5,6},{6,7},{8,9},{9,10},{10,11},{12,13},{... | collective-permute-start | bytes 1253384 | tf_op jit(solution)/shard_map/ppermute | solution.py:972
  219.4 4.4 %ring_add.2 = (bf16[4,48,768]{2,1,0:T(8,128)(2,1)}, bf16[4,48,768]{2,1,0:T(8,128)(2,1)}, bf16[4,48,768]{2,1,0:T(8,128)(2,1)}, bf16[4,48,768]{2,1,0:T(8,128)(2,1)}) custom-call(s32[1]{0:T(128)} %bitcast.13.place, bf16[4,192,768]{2,1,0:T(8,128)(2,1)} %get-tuple-element.173.p0, bf16[4,192,768]{2,1,0:T(8,128)(2,1)} %collective-permute-done.4.p1, ...), custom_call_target="tpu_custom_call" | custom-call | bytes 120000 | tf_op jit(solution)/shard_map/ring_add/pallas_call | solution.py:767
  223.9 5.6 %collective-permute-start.12 = (bf16[4,48,768]{2,1,0:T(8,128)(2,1)}, bf16[4,48,768]{2,1,0:T(8,128)(2,1)}, u32[]{:S(2)}, u32[]{:S(2)}) collective-permute-start(bf16[4,48,768]{2,1,0:T(8,128)(2,1)} %get-tuple-element.185), channel_id=1, source_target_pairs={{0,64},{4,20},{8,72},{12,28},{16,80},{20,4},{24,88},{28,12},{32,96... | collective-permute-start | bytes 884744 | tf_op jit(solution)/shard_map/ppermute | solution.py:945
  229.5 3.4 %ring_add.3 = (bf16[4,32,768]{2,1,0:T(8,128)(2,1)}, bf16[4,32,768]{2,1,0:T(8,128)(2,1)}, bf16[4,32,768]{2,1,0:T(8,128)(2,1)}, bf16[4,32,768]{2,1,0:T(8,128)(2,1)}) custom-call(s32[1]{0:T(128)} %bitcast.13.place, bf16[4,128,768]{2,1,0:T(8,128)(2,1)} %get-tuple-element.178.p0, bf16[4,128,768]{2,1,0:T(8,128)(2,1)} %collective-permute-done.8.p1, ...), custom_call_target="tpu_custom_call" | custom-call | bytes 120000 | tf_op jit(solution)/shard_map/ring_add/pallas_call | solution.py:767
  236.9 3.6 %outgoing_rows.1 = bf16[768,768]{1,0:T(8,128)(2,1)} custom-call(s32[1]{0:T(128)} %bitcast.place, s32[4,1,128]{2,1,0:T(1,128)} %get-tuple-element.187.slot, bf16[272,768]{1,0:T(8,128)(2,1)} %get-tuple-element.199.p0.r0, bf16[272,768]{1,0:T(8,128)(2,1)} %copy-done, bf16[272,768]{1,0:T(8,128)(2,1)} %copy-done.1, bf16[272,768]{1,0:T(8,128)(2,1)} %collective-permute-done.16.p3.r3), custom_call_target="tpu_custom_call" | custom-call | flops 12079595 | bytes 60000 | tf_op jit(solution)/shard_map/outgoing_rows/pallas_call | solution.py:611
  240.6 3.2 reshape.162
  249.1 4.0 %collective-permute-done.20.f1 = bf16[80,768]{1,0:T(8,128)(2,1)S(1)} collective-permute-done((bf16[80,768]{1,0:T(8,128)(2,1)}, bf16[80,768]{1,0:T(8,128)(2,1)S(1)}, u32[]{:S(2)}, u32[]{:S(2)}) %collective-permute-start.20) | collective-permute-done | bytes 122912 | tf_op jit(solution)/shard_map/ppermute | solution.py:949
  266.7 12.1 %all-to-all-start.2 = ((bf16[128,6,768]{2,1,0:T(8,128)(2,1)}), bf16[128,6,768]{2,1,0:T(8,128)(2,1)S(1)}, u32[]{:S(2)}, u32[]{:S(2)}) async-start(bf16[128,6,768]{2,1,0:T(8,128)(2,1)} %reshape.162), calls=%async_computation.2 | async-start | bytes 3145728 | tf_op jit(solution)/shard_map/all_to_all | solution.py:1150
  278.7 2.7 collective-permute-start.28
  282.7 21.0 %all-to-all-done.2 = bf16[128,6,768]{2,1,0:T(8,128)(2,1)S(1)} async-done(((bf16[128,6,768]{2,1,0:T(8,128)(2,1)}), bf16[128,6,768]{2,1,0:T(8,128)(2,1)S(1)}, u32[]{:S(2)}, u32[]{:S(2)}) %all-to-all-start.2) | async-done | bytes 1179680 | tf_op jit(solution)/shard_map/all_to_all | solution.py:1150
  305.8 5.8 %collective-permute-done.26.p1 = bf16[384,768]{1,0:T(8,128)(2,1)} collective-permute-done((bf16[384,768]{1,0:T(8,128)(2,1)S(1)}, bf16[384,768]{1,0:T(8,128)(2,1)}, u32[]{:S(2)}, u32[]{:S(2)}) %collective-permute-start.26) | collective-permute-done | bytes 589856 | tf_op jit(solution)/shard_map/ppermute | solution.py:941
  311.5 3.2 order.3.own
  316.4 8.6 %table_gradient.1 = f32[3912,768]{1,0:T(8,128)} custom-call(s32[1,768]{1,0:T(1,128)} %broadcast_in_dim_reshape.7.fetch, bf16[768,768]{1,0:T(8,128)(2,1)} %reshape.164.incoming), custom_call_target="tpu_custom_call" | custom-call | flops 92295656 | bytes 260000 | tf_op jit(solution)/shard_map/table_gradient/pallas_call | solution.py:634
  325.0 7.4 %finish.1 = (f32[768,768]{1,0:T(8,128)}, f32[192,3072]{1,0:T(8,128)}, f32[192,768]{1,0:T(8,128)}, f32[192,768]{1,0:T(8,128)}, f32[192,768]{1,0:T(8,128)}, /*inde...) custom-call(s32[2]{0:T(128)} %pad_add_fusion.3.place, ...), custom_call_target="tpu_custom_call" | custom-call | bytes 280000 | tf_op jit(solution)/shard_map/finish/pallas_call | solution.py:893
  (140 shorter events, 65.6 us)
Async XLA Ops:
  39.3 29.3 %all-to-all-start.1 = ((bf16[128,6,768]{2,1,0:T(8,128)(2,1)}), bf16[128,6,768]{2,1,0:T(8,128)(2,1)S(1)}, u32[]{:S(2)}, u32[]{:S(2)}) async-start(bf16[128,6,768]{2,1,0:T(8,128)(2,1)} %reshape.149), calls=%async_computation.1 | async-start | bytes 3145728 | tf_op jit(solution)/shard_map/all_to_all | solution.py:1026
  73.3 23.1 %collective-permute-start = (bf16[272,768]{1,0:T(8,128)(2,1)}, bf16[272,768]{1,0:T(8,128)(2,1)S(1)}, u32[]{:S(2)}, u32[]{:S(2)}) collective-permute-start(bf16[272,768]{1,0:T(8,128)(2,1)} %get-tuple-element.123), channel_id=1, source_target_pairs={{0,1},{1,2},{3,0},{4,5},{5,6},{7,4},{8,9},{9,10},{11,8},{12,13},{1... | collective-permute-start | bytes 1253384 | tf_op jit(solution)/shard_map/ppermute | solution.py:964
  75.8 20.6 %collective-permute-start.1 = (bf16[272,768]{1,0:T(8,128)(2,1)}, bf16[272,768]{1,0:T(8,128)(2,1)S(1)}, u32[]{:S(2)}, u32[]{:S(2)}) collective-permute-start(bf16[272,768]{1,0:T(8,128)(2,1)} %get-tuple-element.124), channel_id=1, source_target_pairs={{0,2},{2,0},{3,1},{4,6},{6,4},{7,5},{8,10},{10,8},{11,9},{12,14},{... | collective-permute-start | bytes 1253384 | tf_op jit(solution)/shard_map/ppermute | solution.py:964
  77.7 18.7 %collective-permute-start.2 = (bf16[272,768]{1,0:T(8,128)(2,1)}, bf16[272,768]{1,0:T(8,128)(2,1)}, u32[]{:S(2)}, u32[]{:S(2)}) collective-permute-start(bf16[272,768]{1,0:T(8,128)(2,1)} %get-tuple-element.125), channel_id=1, source_target_pairs={{1,0},{2,1},{3,2},{5,4},{6,5},{7,6},{9,8},{10,9},{11,10},{13,12},{... | collective-permute-start | bytes 1253384 | tf_op jit(solution)/shard_map/ppermute | solution.py:964
  138.9 9.3 %collective-permute-start.3 = (bf16[4,768,768]{2,1,0:T(8,128)(2,1)}, bf16[4,768,768]{2,1,0:T(8,128)(2,1)}, u32[]{:S(2)}, u32[]{:S(2)}) collective-permute-start(bf16[4,768,768]{2,1,0:T(8,128)(2,1)} %ff_send.1), channel_id=1, source_target_pairs={{0,4},{4,0},{8,12},{12,8},{16,20},{20,16},{24,28},{28,24},{32,36},... | collective-permute-start | bytes 14155784 | tf_op jit(solution)/shard_map/ppermute | solution.py:953
  157.4 29.5 %collective-permute-start.4 = (bf16[4,192,768]{2,1,0:T(8,128)(2,1)}, bf16[4,192,768]{2,1,0:T(8,128)(2,1)}, u32[]{:S(2)}, u32[]{:S(2)}) collective-permute-start(bf16[4,192,768]{2,1,0:T(8,128)(2,1)} %get-tuple-element.165), channel_id=1, source_target_pairs={{0,8},{4,36},{8,16},{12,44},{16,24},{20,52},{24,0},{28,60},{32,40}... | collective-permute-start | bytes 3538952 | tf_op jit(solution)/shard_map/ppermute | solution.py:941
  157.8 29.2 %collective-permute-start.5 = (bf16[4,192,768]{2,1,0:T(8,128)(2,1)}, bf16[4,192,768]{2,1,0:T(8,128)(2,1)}, u32[]{:S(2)}, u32[]{:S(2)}) collective-permute-start(bf16[4,192,768]{2,1,0:T(8,128)(2,1)} %get-tuple-element.166), channel_id=1, source_target_pairs={{0,16},{4,68},{8,24},{12,76},{16,0},{20,84},{24,8},{28,92},{32,48}... | collective-permute-start | bytes 3538952 | tf_op jit(solution)/shard_map/ppermute | solution.py:941
  159.4 28.1 %collective-permute-start.6 = (bf16[4,192,768]{2,1,0:T(8,128)(2,1)}, bf16[4,192,768]{2,1,0:T(8,128)(2,1)}, u32[]{:S(2)}, u32[]{:S(2)}) collective-permute-start(bf16[4,192,768]{2,1,0:T(8,128)(2,1)} %get-tuple-element.167), channel_id=1, source_target_pairs={{0,24},{4,100},{8,0},{12,108},{16,8},{20,116},{24,16},{28,124},{32... | collective-permute-start | bytes 3538952 | tf_op jit(solution)/shard_map/ppermute | solution.py:941
  187.6 7.5 %collective-permute-start.7 = (bf16[4,512,768]{2,1,0:T(8,128)(2,1)}, bf16[4,512,768]{2,1,0:T(8,128)(2,1)}, u32[]{:S(2)}, u32[]{:S(2)}) collective-permute-start(bf16[4,512,768]{2,1,0:T(8,128)(2,1)} %get-tuple-element.170), channel_id=1, source_target_pairs={{0,4},{4,0},{8,12},{12,8},{16,20},{20,16},{24,28},{28,24},{32,36},... | collective-permute-start | bytes 9437192 | tf_op jit(solution)/shard_map/ppermute | solution.py:953
  200.2 23.5 %collective-permute-start.8 = (bf16[4,128,768]{2,1,0:T(8,128)(2,1)}, bf16[4,128,768]{2,1,0:T(8,128)(2,1)}, u32[]{:S(2)}, u32[]{:S(2)}) collective-permute-start(bf16[4,128,768]{2,1,0:T(8,128)(2,1)} %get-tuple-element.179), channel_id=1, source_target_pairs={{0,8},{4,36},{8,16},{12,44},{16,24},{20,52},{24,0},{28,60},{32,40}... | collective-permute-start | bytes 2359304 | tf_op jit(solution)/shard_map/ppermute | solution.py:941
  200.6 23.3 %collective-permute-start.9 = (bf16[4,128,768]{2,1,0:T(8,128)(2,1)}, bf16[4,128,768]{2,1,0:T(8,128)(2,1)}, u32[]{:S(2)}, u32[]{:S(2)}) collective-permute-start(bf16[4,128,768]{2,1,0:T(8,128)(2,1)} %get-tuple-element.180), channel_id=1, source_target_pairs={{0,16},{4,68},{8,24},{12,76},{16,0},{20,84},{24,8},{28,92},{32,48}... | collective-permute-start | bytes 2359304 | tf_op jit(solution)/shard_map/ppermute | solution.py:941
  202.3 27.3 %collective-permute-start.10 = (bf16[4,128,768]{2,1,0:T(8,128)(2,1)}, bf16[4,128,768]{2,1,0:T(8,128)(2,1)}, u32[]{:S(2)}, u32[]{:S(2)}) collective-permute-start(bf16[4,128,768]{2,1,0:T(8,128)(2,1)} %get-tuple-element.181), channel_id=1, source_target_pairs={{0,24},{4,100},{8,0},{12,108},{16,8},{20,116},{24,16},{28,124},{32... | collective-permute-start | bytes 2359304 | tf_op jit(solution)/shard_map/ppermute | solution.py:941
  203.0 12.6 %collective-permute-start.14 = (bf16[272,768]{1,0:T(8,128)(2,1)}, bf16[272,768]{1,0:T(8,128)(2,1)S(1)}, u32[]{:S(2)}, u32[]{:S(2)}) collective-permute-start(bf16[272,768]{1,0:T(8,128)(2,1)} %get-tuple-element.188), channel_id=1, source_target_pairs={{1,0},{2,1},{0,3},{5,4},{6,5},{4,7},{9,8},{10,9},{8,11},{13,12},{1... | collective-permute-start | bytes 1253384 | tf_op jit(solution)/shard_map/ppermute | solution.py:972
  205.6 27.3 %collective-permute-start.15 = (bf16[272,768]{1,0:T(8,128)(2,1)}, bf16[272,768]{1,0:T(8,128)(2,1)S(1)}, u32[]{:S(2)}, u32[]{:S(2)}) collective-permute-start(bf16[272,768]{1,0:T(8,128)(2,1)} %get-tuple-element.189), channel_id=1, source_target_pairs={{2,0},{0,2},{1,3},{6,4},{4,6},{5,7},{10,8},{8,10},{9,11},{14,12},{... | collective-permute-start | bytes 1253384 | tf_op jit(solution)/shard_map/ppermute | solution.py:972
  215.6 18.9 %collective-permute-start.16 = (bf16[272,768]{1,0:T(8,128)(2,1)}, bf16[272,768]{1,0:T(8,128)(2,1)}, u32[]{:S(2)}, u32[]{:S(2)}) collective-permute-start(bf16[272,768]{1,0:T(8,128)(2,1)} %get-tuple-element.190), channel_id=1, source_target_pairs={{0,1},{1,2},{2,3},{4,5},{5,6},{6,7},{8,9},{9,10},{10,11},{12,13},{... | collective-permute-start | bytes 1253384 | tf_op jit(solution)/shard_map/ppermute | solution.py:972
  223.8 10.7 %collective-permute-start.11 = (bf16[4,48,768]{2,1,0:T(8,128)(2,1)}, bf16[4,48,768]{2,1,0:T(8,128)(2,1)S(1)}, u32[]{:S(2)}, u32[]{:S(2)}) collective-permute-start(bf16[4,48,768]{2,1,0:T(8,128)(2,1)} %get-tuple-element.184), channel_id=1, source_target_pairs={{0,32},{4,12},{8,40},{12,20},{16,48},{20,28},{24,56},{28,4},{32,64... | collective-permute-start | bytes 884744 | tf_op jit(solution)/shard_map/ppermute | solution.py:945
  223.9 19.9 %collective-permute-start.12 = (bf16[4,48,768]{2,1,0:T(8,128)(2,1)}, bf16[4,48,768]{2,1,0:T(8,128)(2,1)}, u32[]{:S(2)}, u32[]{:S(2)}) collective-permute-start(bf16[4,48,768]{2,1,0:T(8,128)(2,1)} %get-tuple-element.185), channel_id=1, source_target_pairs={{0,64},{4,20},{8,72},{12,28},{16,80},{20,4},{24,88},{28,12},{32,96... | collective-permute-start | bytes 884744 | tf_op jit(solution)/shard_map/ppermute | solution.py:945
  229.5 14.2 %collective-permute-start.13 = (bf16[4,48,768]{2,1,0:T(8,128)(2,1)}, bf16[4,48,768]{2,1,0:T(8,128)(2,1)}, u32[]{:S(2)}, u32[]{:S(2)}) collective-permute-start(bf16[4,48,768]{2,1,0:T(8,128)(2,1)} %get-tuple-element.186), channel_id=1, source_target_pairs={{0,96},{4,28},{8,104},{12,4},{16,112},{20,12},{24,120},{28,20},{32... | collective-permute-start | bytes 884744 | tf_op jit(solution)/shard_map/ppermute | solution.py:945
  232.9 10.9 %collective-permute-start.17 = (bf16[4,32,768]{2,1,0:T(8,128)(2,1)}, bf16[4,32,768]{2,1,0:T(8,128)(2,1)}, u32[]{:S(2)}, u32[]{:S(2)}) collective-permute-start(bf16[4,32,768]{2,1,0:T(8,128)(2,1)} %get-tuple-element.192), channel_id=1, source_target_pairs={{0,32},{4,12},{8,40},{12,20},{16,48},{20,28},{24,56},{28,4},{32,64... | collective-permute-start | bytes 589832 | tf_op jit(solution)/shard_map/ppermute | solution.py:945
  234.4 9.3 %collective-permute-start.18 = (bf16[4,32,768]{2,1,0:T(8,128)(2,1)}, bf16[4,32,768]{2,1,0:T(8,128)(2,1)}, u32[]{:S(2)}, u32[]{:S(2)}) collective-permute-start(bf16[4,32,768]{2,1,0:T(8,128)(2,1)} %get-tuple-element.193), channel_id=1, source_target_pairs={{0,64},{4,20},{8,72},{12,28},{16,80},{20,4},{24,88},{28,12},{32,96... | collective-permute-start | bytes 589832 | tf_op jit(solution)/shard_map/ppermute | solution.py:945
  234.5 9.3 %collective-permute-start.19 = (bf16[4,32,768]{2,1,0:T(8,128)(2,1)}, bf16[4,32,768]{2,1,0:T(8,128)(2,1)}, u32[]{:S(2)}, u32[]{:S(2)}) collective-permute-start(bf16[4,32,768]{2,1,0:T(8,128)(2,1)} %get-tuple-element.194), channel_id=1, source_target_pairs={{0,96},{4,28},{8,104},{12,4},{16,112},{20,12},{24,120},{28,20},{32... | collective-permute-start | bytes 589832 | tf_op jit(solution)/shard_map/ppermute | solution.py:945
  246.4 6.7 %collective-permute-start.20 = (bf16[80,768]{1,0:T(8,128)(2,1)}, bf16[80,768]{1,0:T(8,128)(2,1)S(1)}, u32[]{:S(2)}, u32[]{:S(2)}) collective-permute-start(bf16[80,768]{1,0:T(8,128)(2,1)} %get-tuple-element.196), channel_id=1, source_target_pairs={{0,1},{1,2},{2,3},{3,0},{4,5},{5,6},{6,7},{7,4},{8,9},{9,10},{10,1... | collective-permute-start | bytes 368648 | tf_op jit(solution)/shard_map/ppermute | solution.py:949
  246.4 6.7 %collective-permute-start.21 = (bf16[80,768]{1,0:T(8,128)(2,1)}, bf16[80,768]{1,0:T(8,128)(2,1)S(1)}, u32[]{:S(2)}, u32[]{:S(2)}) collective-permute-start(bf16[80,768]{1,0:T(8,128)(2,1)} %get-tuple-element.197), channel_id=1, source_target_pairs={{0,2},{1,3},{2,0},{3,1},{4,6},{5,7},{6,4},{7,5},{8,10},{9,11},{10,... | collective-permute-start | bytes 368648 | tf_op jit(solution)/shard_map/ppermute | solution.py:949
  246.8 6.9 %collective-permute-start.22 = (bf16[80,768]{1,0:T(8,128)(2,1)}, bf16[80,768]{1,0:T(8,128)(2,1)S(1)}, u32[]{:S(2)}, u32[]{:S(2)}) collective-permute-start(bf16[80,768]{1,0:T(8,128)(2,1)} %get-tuple-element.198), channel_id=1, source_target_pairs={{0,3},{1,0},{2,1},{3,2},{4,7},{5,4},{6,5},{7,6},{8,11},{9,8},{10,9... | collective-permute-start | bytes 368648 | tf_op jit(solution)/shard_map/ppermute | solution.py:949
  256.3 6.9 %collective-permute-start.25 = (bf16[96,768]{1,0:T(8,128)(2,1)}, bf16[96,768]{1,0:T(8,128)(2,1)S(1)}, u32[]{:S(2)}, u32[]{:S(2)}) collective-permute-start(bf16[96,768]{1,0:T(8,128)(2,1)} %piece_rows.1.p0), channel_id=1, source_target_pairs={{0,96},{4,28},{8,104},{12,4},{16,112},{20,12},{24,120},{28,20},{32... | collective-permute-start | bytes 442376 | tf_op jit(solution)/shard_map/ppermute | solution.py:945
  256.7 6.5 %collective-permute-start.24 = (bf16[96,768]{1,0:T(8,128)(2,1)}, bf16[96,768]{1,0:T(8,128)(2,1)S(1)}, u32[]{:S(2)}, u32[]{:S(2)}) collective-permute-start(bf16[96,768]{1,0:T(8,128)(2,1)} %piece_rows.1.p0), channel_id=1, source_target_pairs={{0,64},{4,20},{8,72},{12,28},{16,80},{20,4},{24,88},{28,12},{32,96... | collective-permute-start | bytes 442376 | tf_op jit(solution)/shard_map/ppermute | solution.py:945
  257.4 6.7 %collective-permute-start.23 = (bf16[96,768]{1,0:T(8,128)(2,1)}, bf16[96,768]{1,0:T(8,128)(2,1)S(1)}, u32[]{:S(2)}, u32[]{:S(2)}) collective-permute-start(bf16[96,768]{1,0:T(8,128)(2,1)} %piece_rows.1.p0), channel_id=1, source_target_pairs={{0,32},{4,12},{8,40},{12,20},{16,48},{20,28},{24,56},{28,4},{32,64... | collective-permute-start | bytes 442376 | tf_op jit(solution)/shard_map/ppermute | solution.py:945
  266.7 37.0 %all-to-all-start.2 = ((bf16[128,6,768]{2,1,0:T(8,128)(2,1)}), bf16[128,6,768]{2,1,0:T(8,128)(2,1)S(1)}, u32[]{:S(2)}, u32[]{:S(2)}) async-start(bf16[128,6,768]{2,1,0:T(8,128)(2,1)} %reshape.162), calls=%async_computation.2 | async-start | bytes 3145728 | tf_op jit(solution)/shard_map/all_to_all | solution.py:1150
  278.7 26.2 %collective-permute-start.28 = (bf16[384,768]{1,0:T(8,128)(2,1)S(1)}, bf16[384,768]{1,0:T(8,128)(2,1)S(1)}, u32[]{:S(2)}, u32[]{:S(2)}) collective-permute-start(bf16[384,768]{1,0:T(8,128)(2,1)S(1)} %bitcast.32), channel_id=1, source_target_pairs={{0,24},{4,100},{8,0},{12,108},{16,8},{20,116},{24,16},{28,124},{32... | collective-permute-start | bytes 1769480 | tf_op jit(solution)/shard_map/ppermute | solution.py:941
  281.5 24.0 %collective-permute-start.27 = (bf16[384,768]{1,0:T(8,128)(2,1)S(1)}, bf16[384,768]{1,0:T(8,128)(2,1)}, u32[]{:S(2)}, u32[]{:S(2)}) collective-permute-start(bf16[384,768]{1,0:T(8,128)(2,1)S(1)} %bitcast.33), channel_id=1, source_target_pairs={{0,16},{4,68},{8,24},{12,76},{16,0},{20,84},{24,8},{28,92},{32,48}... | collective-permute-start | bytes 1769480 | tf_op jit(solution)/shard_map/ppermute | solution.py:941
  282.1 29.4 %collective-permute-start.26 = (bf16[384,768]{1,0:T(8,128)(2,1)S(1)}, bf16[384,768]{1,0:T(8,128)(2,1)}, u32[]{:S(2)}, u32[]{:S(2)}) collective-permute-start(bf16[384,768]{1,0:T(8,128)(2,1)S(1)} %bitcast.34), channel_id=1, source_target_pairs={{0,8},{4,36},{8,16},{12,44},{16,24},{20,52},{24,0},{28,60},{32,40}... | collective-permute-start | bytes 1769480 | tf_op jit(solution)/shard_map/ppermute | solution.py:941
  314.7 10.3 %collective-permute-start.29 = (bf16[4,384,768]{2,1,0:T(8,128)(2,1)}, bf16[4,384,768]{2,1,0:T(8,128)(2,1)}, u32[]{:S(2)}, u32[]{:S(2)}) collective-permute-start(bf16[4,384,768]{2,1,0:T(8,128)(2,1)} %order.3.own), channel_id=1, source_target_pairs={{0,4},{4,0},{8,12},{12,8},{16,20},{20,16},{24,28},{28,24},{32,36},... | collective-permute-start | bytes 7077896 | tf_op jit(solution)/shard_map/ppermute | solution.py:953
  (25 other events, 131.2 us)
